TPU v7x, 256 devices: a whole 4x4x8 slice. The times are simulated.
256 devices in a mesh: dp: 32 (over y_lo, z, core), space: 8 (over x, y_hi).
Axes of the slice: x: 4, y: 4 (y_hi: 2, y_lo: 2; y = y_hi * 2 + y_lo), z: 8, core: 2. Of those that a mesh axis runs over, the one named last changes fastest.
Arguments:
- volumes: bfloat16 [32, 32, 32, 8, 128], P('dp', None, 'space'), may hold values from -6 to 6
- w_first: bfloat16 [864, 64], P('dp'), may hold values from -0.21875 to 0.21875
- w_second: bfloat16 [1728, 128], P('dp'), may hold values from -0.4375 to 0.4375
- cotangent: bfloat16 [32, 128, 8, 2, 32], P('dp', None, 'space'), may hold values from -96 to 96
Outputs:
- pooled: bfloat16 [32, 128, 8, 2, 32], P('dp', None, 'space')
- volume_grad: bfloat16 [32, 32, 32, 8, 128], P('dp', None, 'space')
- grad_first: float32 [864, 64], P('dp')
- grad_second: float32 [1728, 128], P('dp')
All inputs are finite; a program needn't handle non-finite values.
Results may differ from a plain program's by a relative error of at most 0.023.
Values may be sent and summed in bfloat16 or wider, within the bound.
A program may use at most 128 MiB of HBM per device.

v0:
```python
import jax
import jax.numpy as jnp
from jax import lax
from jax.sharding import PartitionSpec as P


def with_halo(block, sides, width):
    for axis, dim in sides:
        count = lax.axis_size(axis)
        forward = [(i, i + 1) for i in range(count - 1)]
        backward = [(target, source) for source, target in forward]
        low = lax.ppermute(
            lax.slice_in_dim(block, block.shape[dim] - width, None, axis=dim), axis, forward
        )
        high = lax.ppermute(lax.slice_in_dim(block, 0, width, axis=dim), axis, backward)
        block = jnp.concatenate([low, block, high], axis=dim)
    return block


def pad_sides(field):
    return jnp.pad(field, ((0, 0), (0, 0), (0, 0), (1, 1), (1, 1)))


def conv_forward(padded, weight):
    samples_here, in_width, depth_padded, extent_y, extent_z = padded.shape
    extent_x = depth_padded - 2
    out_width = weight.shape[1]
    framed = pad_sides(padded)
    kernel = weight.reshape(3, 3, 3, in_width, out_width)
    summed = jnp.zeros((samples_here, out_width, extent_x, extent_y, extent_z), jnp.float32)
    for along_x in range(3):
        for along_y in range(3):
            for along_z in range(3):
                window = framed[
                    :,
                    :,
                    along_x : along_x + extent_x,
                    along_y : along_y + extent_y,
                    along_z : along_z + extent_z,
                ]
                summed = summed + jnp.einsum(
                    "sixyz,io->soxyz",
                    window,
                    kernel[along_x, along_y, along_z],
                    preferred_element_type=jnp.float32,
                )
    return summed


def conv_input_grad(padded, weight, in_width):
    samples_here, out_width, depth_padded, extent_y, extent_z = padded.shape
    extent_x = depth_padded - 2
    framed = pad_sides(padded)
    kernel = weight.reshape(3, 3, 3, in_width, out_width)
    summed = jnp.zeros((samples_here, in_width, extent_x, extent_y, extent_z), jnp.float32)
    for along_x in range(3):
        for along_y in range(3):
            for along_z in range(3):
                window = framed[
                    :,
                    :,
                    2 - along_x : 2 - along_x + extent_x,
                    2 - along_y : 2 - along_y + extent_y,
                    2 - along_z : 2 - along_z + extent_z,
                ]
                summed = summed + jnp.einsum(
                    "soxyz,io->sixyz",
                    window,
                    kernel[along_x, along_y, along_z],
                    preferred_element_type=jnp.float32,
                )
    return summed


def conv_weight_grad(padded, grads):
    samples_here, in_width, depth_padded, extent_y, extent_z = padded.shape
    extent_x = depth_padded - 2
    framed = pad_sides(padded)
    pieces = []
    for along_x in range(3):
        for along_y in range(3):
            for along_z in range(3):
                window = framed[
                    :,
                    :,
                    along_x : along_x + extent_x,
                    along_y : along_y + extent_y,
                    along_z : along_z + extent_z,
                ]
                pieces.append(
                    jnp.einsum("sixyz,soxyz->io", window, grads, preferred_element_type=jnp.float32)
                )
    return jnp.stack(pieces).reshape(27 * in_width, grads.shape[1])


def pooling(field):
    samples_here, width, extent_x, extent_y, extent_z = field.shape
    blocks = field.reshape(
        samples_here, width, extent_x // 2, 2, extent_y // 2, 2, extent_z // 2, 2
    )
    return jnp.mean(blocks, axis=(3, 5, 7))


def spread_up(field):
    samples_here, width, extent_x, extent_y, extent_z = field.shape
    blocks = jnp.broadcast_to(
        field[:, :, :, None, :, None, :, None],
        (samples_here, width, extent_x, 2, extent_y, 2, extent_z, 2),
    )
    return blocks.reshape(samples_here, width, 2 * extent_x, 2 * extent_y, 2 * extent_z)


def silu_slope(values):
    sigma = jax.nn.sigmoid(values)
    return sigma * (1.0 + values * (1.0 - sigma))


def local(volumes, w_first, w_second, cotangent):
    kernel_one, kernel_two = (
        lax.all_gather(w_first, "dp", axis=0, tiled=True),
        lax.all_gather(w_second, "dp", axis=0, tiled=True),
    )
    in_width = volumes.shape[1]
    mid_width = kernel_one.shape[1]
    count_one = lax.axis_size("dp") * lax.axis_size("space") * (volumes.size // in_width)
    factor_one = float(count_one) ** (-0.5)
    factor_two = float(count_one // 8) ** (-0.5)
    input_padded = with_halo(volumes, (("space", 2),), 1)
    first_pre = conv_forward(input_padded, kernel_one)
    first_pool = pooling(jax.nn.silu(first_pre)).astype(jnp.bfloat16)
    pool_padded = with_halo(first_pool, (("space", 2),), 1)
    second_pre = conv_forward(pool_padded, kernel_two)
    pooled = pooling(jax.nn.silu(second_pre)).astype(jnp.bfloat16)
    second_delta = (
        spread_up(cotangent.astype(jnp.float32)) * 0.125 * silu_slope(second_pre)
    ).astype(jnp.bfloat16)
    grad_two = conv_weight_grad(pool_padded, second_delta) * factor_two
    delta_padded = with_halo(second_delta, (("space", 2),), 1)
    pool_grad = conv_input_grad(delta_padded, kernel_two, mid_width).astype(jnp.bfloat16)
    first_delta = (spread_up(pool_grad.astype(jnp.float32)) * 0.125 * silu_slope(first_pre)).astype(
        jnp.bfloat16
    )
    grad_one = conv_weight_grad(input_padded, first_delta) * factor_one
    first_padded = with_halo(first_delta, (("space", 2),), 1)
    volume_grad = conv_input_grad(first_padded, kernel_one, in_width).astype(jnp.bfloat16)
    rows_one, rows_two = (
        lax.psum_scatter(
            grad_one.astype(jnp.bfloat16), "dp", scatter_dimension=0, tiled=True
        ).astype(jnp.float32),
        lax.psum_scatter(
            grad_two.astype(jnp.bfloat16), "dp", scatter_dimension=0, tiled=True
        ).astype(jnp.float32),
    )
    share_one, share_two = (
        lax.psum(rows_one.astype(jnp.bfloat16), "space").astype(jnp.float32),
        lax.psum(rows_two.astype(jnp.bfloat16), "space").astype(jnp.float32),
    )
    return (pooled, volume_grad, share_one, share_two)


def solution(mesh):
    return jax.shard_map(
        local,
        mesh=mesh,
        in_specs=(
            P("dp", None, "space", None, None),
            P("dp", None),
            P("dp", None),
            P("dp", None, "space", None, None),
        ),
        out_specs=(
            P("dp", None, "space", None, None),
            P("dp", None, "space", None, None),
            P("dp", None),
            P("dp", None),
        ),
        check_vma=False,
    )
```

profile of v0, /device:TPU:32, one launch (start us, length us, event | category | flops | bytes accessed | tf_op | source)
XLA Modules:
  0.0 299.0 jit_solution(13379880427681601026)
XLA Ops:
  0.6 1.1 copy.81
  1.7 5.1 %collective-permute-start = (bf16[1,32,1,8,128]{4,1,3,2,0:T(8,128)(2,1)S(1)}, bf16[1,32,1,8,128]{4,1,3,2,0:T(8,128)(2,1)S(1)}, u32[]{:S(2)}, u32[]{:S(2)}) collective-permute-start(bf16[1,32,1,8,128]{4,1,3,2,0:T(8,128)(2,1)S(1)} %get-tuple-element.26), channel_id=1, source_target_pairs={{0,1},{1,2},{2,3},{3,4},{4,5},{5,6},{6,7},{8,9},{9,10},{10,11},{11... | collective-permute-start | bytes 196616 | tf_op jit(solution)/shard_map/ppermute | solution.py:12
  6.8 1.3 collective-permute-start.1
  8.1 0.7 multiply_bitcast_fusion
  8.8 34.2 %all-gather = bf16[32,27,64]{2,1,0:T(8,128)(2,1)S(1)} all-gather(bf16[1,27,64]{2,1,0:T(8,128)(2,1)} %bitcast.1526), channel_id=1, replica_groups=mesh['dp'=32,'space'=8] {'dp'}, dimensions={0}, use_global_device_ids=true | all-gather | bytes 114048 | tf_op jit(solution)/shard_map/all_gather | solution.py:120
  43.2 0.4 select_maximum_fusion.2
  46.5 0.4 convolution_bitcast_fusion
  48.4 0.4 convolution_add_fusion.10
  50.9 0.4 convolution_add_fusion.3
  52.6 0.6 fusion.17
  53.6 2.0 fusion.134
  55.5 1.8 copy.87
  57.4 2.4 reduce_sum.21
  59.8 1.0 fusion.210
  60.8 6.7 %collective-permute-start.2 = (bf16[1,64,1,4,64]{1,4,3,2,0:T(8,128)(2,1)S(1)}, bf16[1,64,1,4,64]{1,4,3,2,0:T(8,128)(2,1)S(1)}, u32[]{:S(2)}, u32[]{:S(2)}) collective-permute-start(bf16[1,64,1,4,64]{1,4,3,2,0:T(8,128)(2,1)S(1)} %get-tuple-element.30), channel_id=1, source_target_pairs={{0,1},{1,2},{2,3},{3,4},{4,5},{5,6},{6,7},{8,9},{9,10},{10,11},{11... | collective-permute-start | bytes 98312 | tf_op jit(solution)/shard_map/ppermute | solution.py:12
  67.5 1.3 collective-permute-start.3
  68.8 35.1 %all-gather.1 = bf16[32,54,128]{2,1,0:T(8,128)(2,1)S(1)} all-gather(bf16[1,54,128]{2,1,0:T(8,128)(2,1)S(1)} %bitcast.1525), channel_id=1, replica_groups=mesh['dp'=32,'space'=8] {'dp'}, dimensions={0}, use_global_device_ids=true | all-gather | bytes 456192 | tf_op jit(solution)/shard_map/all_gather | solution.py:121
  104.0 0.6 dynamic-slice.6
  116.6 0.9 multiply_convert_fusion.1
  117.5 5.9 %collective-permute-start.4 = (bf16[1,128,1,4,64]{1,4,3,2,0:T(8,128)(2,1)S(1)}, bf16[1,128,1,4,64]{1,4,3,2,0:T(8,128)(2,1)S(1)}, u32[]{:S(2)}, u32[]{:S(2)}) collective-permute-start(bf16[1,128,1,4,64]{1,4,3,2,0:T(8,128)(2,1)S(1)} %get-tuple-element.28), channel_id=1, source_target_pairs={{0,1},{1,2},{2,3},{3,4},{4,5},{5,6},{6,7},{8,9},{9,10},{10,11},{11... | collective-permute-start | bytes 196616 | tf_op jit(solution)/shard_map/ppermute | solution.py:12
  123.5 1.3 collective-permute-start.5
  124.9 0.6 fusion.196
  125.5 5.7 %collective-permute-done.5 = bf16[1,128,1,4,64]{1,4,3,2,0:T(8,128)(2,1)S(1)} collective-permute-done((bf16[1,128,1,4,64]{1,4,3,2,0:T(8,128)(2,1)S(1)}, bf16[1,128,1,4,64]{1,4,3,2,0:T(8,128)(2,1)S(1)}, u32[]{:S(2)}, u32[]{:S(2)}) %collective-permute-start.5) | collective-permute-done | bytes 65568 | tf_op jit(solution)/shard_map/ppermute | solution.py:15
  136.1 0.9 broadcast_in_dim.16
  137.0 1.6 copy.88
  138.6 1.9 multiply_convert_fusion
  148.8 53.5 %fusion.211 = (bf16[32,64]{1,0:T(8,128)(2,1)S(1)}, bf16[64,128]{1,0:T(8,128)(2,1)S(1)}) fusion(bf16[864,64]{1,0:T(8,128)(2,1)S(1)} %bitcast.1522, bf16[1728,128]{1,0:T(8,128)(2,1)S(1)} %bitcast.1521), kind=kCustom, calls=%all-reduce-scatter.2 | all-reduce-scatter fusion | flops 327682 | bytes 574464
  202.3 1.3 collective-permute-start.10
  203.6 1.3 collective-permute-start.11
  204.9 1.9 collective-permute-start.8
  206.9 8.5 %collective-permute-start.12 = (bf16[27,64]{1,0:T(8,128)(2,1)S(1)}, bf16[27,64]{1,0:T(8,128)(2,1)S(1)}, u32[]{:S(2)}, u32[]{:S(2)}) collective-permute-start(bf16[27,64]{1,0:T(8,128)(2,1)S(1)} %slice.954), channel_id=1, source_target_pairs={{0,40},{8,48},{16,56},{24,64},{32,72},{40,80},{48,88},{56,96},{64,... | collective-permute-start | bytes 10376
  215.6 5.7 %collective-permute-start.13 = (bf16[64,128]{1,0:T(8,128)(2,1)S(1)}, bf16[64,128]{1,0:T(8,128)(2,1)S(1)}, u32[]{:S(2)}, u32[]{:S(2)}) collective-permute-start(bf16[64,128]{1,0:T(8,128)(2,1)S(1)} %get-tuple-element.21), channel_id=1, source_target_pairs={{0,8},{8,16},{16,24},{24,32},{32,40},{40,48},{48,56},{56,64},{64,7... | collective-permute-start | bytes 49160
  221.3 2.0 collective-permute-start.9
  223.3 4.6 %collective-permute-start.17 = (bf16[54,128]{1,0:T(8,128)(2,1)S(1)}, bf16[54,128]{1,0:T(8,128)(2,1)S(1)}, u32[]{:S(2)}, u32[]{:S(2)}) collective-permute-start(bf16[54,128]{1,0:T(8,128)(2,1)S(1)} %slice.955), channel_id=1, source_target_pairs={{0,40},{8,48},{16,56},{24,64},{32,72},{40,80},{48,88},{56,96},{64,... | collective-permute-start | bytes 41480
  228.0 2.8 collective-permute-start.14
  230.7 2.7 collective-permute-start.15
  233.4 3.3 %collective-permute-start.16 = (bf16[64,128]{1,0:T(8,128)(2,1)S(1)}, bf16[64,128]{1,0:T(8,128)(2,1)S(1)}, u32[]{:S(2)}, u32[]{:S(2)}) collective-permute-start(bf16[64,128]{1,0:T(8,128)(2,1)S(1)} %get-tuple-element.21), channel_id=1, source_target_pairs={{0,32},{8,40},{16,48},{24,56},{32,64},{40,72},{48,80},{56,88},{64,... | collective-permute-start | bytes 49160
  236.7 0.7 concatenate.48
  237.4 1.3 collective-permute-start.7
  238.7 6.8 %collective-permute-start.6 = (bf16[1,64,1,8,128]{4,1,3,2,0:T(8,128)(2,1)S(1)}, bf16[1,64,1,8,128]{4,1,3,2,0:T(8,128)(2,1)S(1)}, u32[]{:S(2)}, u32[]{:S(2)}) collective-permute-start(bf16[1,64,1,8,128]{4,1,3,2,0:T(8,128)(2,1)S(1)} %get-tuple-element.22), channel_id=1, source_target_pairs={{0,1},{1,2},{2,3},{3,4},{4,5},{5,6},{6,7},{8,9},{9,10},{10,11},{11... | collective-permute-start | bytes 393224 | tf_op jit(solution)/shard_map/ppermute | solution.py:12
  245.5 0.9 concatenate.49
  246.5 41.0 %all-reduce.8 = (bf16[27,64]{1,0:T(8,128)(2,1)S(1)}, bf16[54,128]{1,0:T(8,128)(2,1)S(1)}) all-reduce(bf16[27,64]{1,0:T(8,128)(2,1)S(1)} %constant_dynamic-slice_fusion.1, bf16[54,128]{1,0:T(8,128)(2,1)S(1)} %constant_dynamic-slice_fusion), channel_id=1, replica_groups=mesh['dp'=32,'space'=8] {'space'}, use_global_device_ids=true, to_apply=%region_4.5 | all-reduce | flops 8640 | bytes 34560 | tf_op jit(solution)/shard_map/psum | solution.py:155
  287.5 0.6 convert_element_type.112
  288.1 0.6 convert_element_type.109
  288.7 1.1 select_maximum_fusion
  296.6 0.6 fusion.50
  297.6 0.5 fusion.76
  298.1 0.8 copy.117
  (203 shorter events, 39.2 us)
Async XLA Ops:
  1.7 41.4 %collective-permute-start = (bf16[1,32,1,8,128]{4,1,3,2,0:T(8,128)(2,1)S(1)}, bf16[1,32,1,8,128]{4,1,3,2,0:T(8,128)(2,1)S(1)}, u32[]{:S(2)}, u32[]{:S(2)}) collective-permute-start(bf16[1,32,1,8,128]{4,1,3,2,0:T(8,128)(2,1)S(1)} %get-tuple-element.26), channel_id=1, source_target_pairs={{0,1},{1,2},{2,3},{3,4},{4,5},{5,6},{6,7},{8,9},{9,10},{10,11},{11... | collective-permute-start | bytes 196616 | tf_op jit(solution)/shard_map/ppermute | solution.py:12
  6.8 36.3 %collective-permute-start.1 = (bf16[1,32,1,8,128]{4,1,3,2,0:T(8,128)(2,1)S(1)}, bf16[1,32,1,8,128]{4,1,3,2,0:T(8,128)(2,1)S(1)}, u32[]{:S(2)}, u32[]{:S(2)}) collective-permute-start(bf16[1,32,1,8,128]{4,1,3,2,0:T(8,128)(2,1)S(1)} %get-tuple-element.27), channel_id=1, source_target_pairs={{1,0},{2,1},{3,2},{4,3},{5,4},{6,5},{7,6},{9,8},{10,9},{11,10},{12... | collective-permute-start | bytes 196616 | tf_op jit(solution)/shard_map/ppermute | solution.py:15
  43.1 10.5 %copy-start.3 = (bf16[3,3,3,32,64]{4,3,2,1,0:T(8,128)(2,1)}, bf16[3,3,3,32,64]{4,3,2,1,0:T(8,128)(2,1)S(1)}, u32[]{:S(2)}) copy-start(bf16[3,3,3,32,64]{4,3,2,1,0:T(8,128)(2,1)S(1)} %reshape.915) | copy-start | bytes 331780
  51.3 1.0 copy-start.1
  57.4 11.4 %copy-start.6 = (bf16[54,128]{1,0:T(8,128)(2,1)S(1)}, bf16[54,128]{1,0:T(8,128)(2,1)}, u32[]{:S(2)}) copy-start(bf16[54,128]{1,0:T(8,128)(2,1)} %param.6) | copy-start | bytes 41476
  57.4 46.6 %copy-start.7 = (u32[256]{0:T(256)S(1)}, u32[256]{0:T(256)}, u32[]{:S(2)}) copy-start(u32[256]{0:T(256)} %constant.37) | copy-start | bytes 3076
  60.8 45.1 %collective-permute-start.2 = (bf16[1,64,1,4,64]{1,4,3,2,0:T(8,128)(2,1)S(1)}, bf16[1,64,1,4,64]{1,4,3,2,0:T(8,128)(2,1)S(1)}, u32[]{:S(2)}, u32[]{:S(2)}) collective-permute-start(bf16[1,64,1,4,64]{1,4,3,2,0:T(8,128)(2,1)S(1)} %get-tuple-element.30), channel_id=1, source_target_pairs={{0,1},{1,2},{2,3},{3,4},{4,5},{5,6},{6,7},{8,9},{9,10},{10,11},{11... | collective-permute-start | bytes 98312 | tf_op jit(solution)/shard_map/ppermute | solution.py:12
  67.5 38.4 %collective-permute-start.3 = (bf16[1,64,1,4,64]{1,4,3,2,0:T(8,128)(2,1)S(1)}, bf16[1,64,1,4,64]{1,4,3,2,0:T(8,128)(2,1)S(1)}, u32[]{:S(2)}, u32[]{:S(2)}) collective-permute-start(bf16[1,64,1,4,64]{1,4,3,2,0:T(8,128)(2,1)S(1)} %get-tuple-element.31), channel_id=1, source_target_pairs={{1,0},{2,1},{3,2},{4,3},{5,4},{6,5},{7,6},{9,8},{10,9},{11,10},{12... | collective-permute-start | bytes 98312 | tf_op jit(solution)/shard_map/ppermute | solution.py:15
  107.7 1.0 copy-start
  117.5 8.0 %collective-permute-start.4 = (bf16[1,128,1,4,64]{1,4,3,2,0:T(8,128)(2,1)S(1)}, bf16[1,128,1,4,64]{1,4,3,2,0:T(8,128)(2,1)S(1)}, u32[]{:S(2)}, u32[]{:S(2)}) collective-permute-start(bf16[1,128,1,4,64]{1,4,3,2,0:T(8,128)(2,1)S(1)} %get-tuple-element.28), channel_id=1, source_target_pairs={{0,1},{1,2},{2,3},{3,4},{4,5},{5,6},{6,7},{8,9},{9,10},{10,11},{11... | collective-permute-start | bytes 196616 | tf_op jit(solution)/shard_map/ppermute | solution.py:12
  123.5 7.7 %collective-permute-start.5 = (bf16[1,128,1,4,64]{1,4,3,2,0:T(8,128)(2,1)S(1)}, bf16[1,128,1,4,64]{1,4,3,2,0:T(8,128)(2,1)S(1)}, u32[]{:S(2)}, u32[]{:S(2)}) collective-permute-start(bf16[1,128,1,4,64]{1,4,3,2,0:T(8,128)(2,1)S(1)} %get-tuple-element.29), channel_id=1, source_target_pairs={{1,0},{2,1},{3,2},{4,3},{5,4},{6,5},{7,6},{9,8},{10,9},{11,10},{12... | collective-permute-start | bytes 196616 | tf_op jit(solution)/shard_map/ppermute | solution.py:15
  142.9 1.5 copy-start.2
  147.5 1.3 copy-start.5
  147.8 67.6 %copy-start.4 = (bf16[3,3,3,32,64]{4,3,2,1,0:T(8,128)(2,1)S(1)}, bf16[3,3,3,32,64]{4,3,2,1,0:T(8,128)(2,1)}, u32[]{:S(2)}) copy-start(bf16[3,3,3,32,64]{4,3,2,1,0:T(8,128)(2,1)} %copy-done.3) | copy-start | bytes 331780
  202.3 21.0 %collective-permute-start.10 = (bf16[32,64]{1,0:T(8,128)(2,1)S(1)}, bf16[32,64]{1,0:T(8,128)(2,1)S(1)}, u32[]{:S(2)}, u32[]{:S(2)}) collective-permute-start(bf16[32,64]{1,0:T(8,128)(2,1)S(1)} %get-tuple-element.20), channel_id=1, source_target_pairs={{0,24},{8,32},{16,40},{24,48},{32,56},{40,64},{48,72},{56,80},{64,... | collective-permute-start | bytes 12296
  203.6 24.3 %collective-permute-start.11 = (bf16[32,64]{1,0:T(8,128)(2,1)S(1)}, bf16[32,64]{1,0:T(8,128)(2,1)S(1)}, u32[]{:S(2)}, u32[]{:S(2)}) collective-permute-start(bf16[32,64]{1,0:T(8,128)(2,1)S(1)} %get-tuple-element.20), channel_id=1, source_target_pairs={{0,32},{8,40},{16,48},{24,56},{32,64},{40,72},{48,80},{56,88},{64,... | collective-permute-start | bytes 12296
  204.9 25.8 %collective-permute-start.8 = (bf16[32,64]{1,0:T(8,128)(2,1)S(1)}, bf16[32,64]{1,0:T(8,128)(2,1)S(1)}, u32[]{:S(2)}, u32[]{:S(2)}) collective-permute-start(bf16[32,64]{1,0:T(8,128)(2,1)S(1)} %get-tuple-element.20), channel_id=1, source_target_pairs={{0,8},{8,16},{16,24},{24,32},{32,40},{40,48},{48,56},{56,64},{64,7... | collective-permute-start | bytes 12296
  206.9 14.4 %collective-permute-start.12 = (bf16[27,64]{1,0:T(8,128)(2,1)S(1)}, bf16[27,64]{1,0:T(8,128)(2,1)S(1)}, u32[]{:S(2)}, u32[]{:S(2)}) collective-permute-start(bf16[27,64]{1,0:T(8,128)(2,1)S(1)} %slice.954), channel_id=1, source_target_pairs={{0,40},{8,48},{16,56},{24,64},{32,72},{40,80},{48,88},{56,96},{64,... | collective-permute-start | bytes 10376
  215.6 23.1 %collective-permute-start.13 = (bf16[64,128]{1,0:T(8,128)(2,1)S(1)}, bf16[64,128]{1,0:T(8,128)(2,1)S(1)}, u32[]{:S(2)}, u32[]{:S(2)}) collective-permute-start(bf16[64,128]{1,0:T(8,128)(2,1)S(1)} %get-tuple-element.21), channel_id=1, source_target_pairs={{0,8},{8,16},{16,24},{24,32},{32,40},{40,48},{48,56},{56,64},{64,7... | collective-permute-start | bytes 49160
  221.3 12.1 %collective-permute-start.9 = (bf16[32,64]{1,0:T(8,128)(2,1)S(1)}, bf16[32,64]{1,0:T(8,128)(2,1)S(1)}, u32[]{:S(2)}, u32[]{:S(2)}) collective-permute-start(bf16[32,64]{1,0:T(8,128)(2,1)S(1)} %get-tuple-element.20), channel_id=1, source_target_pairs={{0,16},{8,24},{16,32},{24,40},{32,48},{40,56},{48,64},{56,72},{64,... | collective-permute-start | bytes 12296
  223.3 14.1 %collective-permute-start.17 = (bf16[54,128]{1,0:T(8,128)(2,1)S(1)}, bf16[54,128]{1,0:T(8,128)(2,1)S(1)}, u32[]{:S(2)}, u32[]{:S(2)}) collective-permute-start(bf16[54,128]{1,0:T(8,128)(2,1)S(1)} %slice.955), channel_id=1, source_target_pairs={{0,40},{8,48},{16,56},{24,64},{32,72},{40,80},{48,88},{56,96},{64,... | collective-permute-start | bytes 41480
  228.0 17.5 %collective-permute-start.14 = (bf16[64,128]{1,0:T(8,128)(2,1)S(1)}, bf16[64,128]{1,0:T(8,128)(2,1)S(1)}, u32[]{:S(2)}, u32[]{:S(2)}) collective-permute-start(bf16[64,128]{1,0:T(8,128)(2,1)S(1)} %get-tuple-element.21), channel_id=1, source_target_pairs={{0,16},{8,24},{16,32},{24,40},{32,48},{40,56},{48,64},{56,72},{64,... | collective-permute-start | bytes 49160
  230.7 14.8 %collective-permute-start.15 = (bf16[64,128]{1,0:T(8,128)(2,1)S(1)}, bf16[64,128]{1,0:T(8,128)(2,1)S(1)}, u32[]{:S(2)}, u32[]{:S(2)}) collective-permute-start(bf16[64,128]{1,0:T(8,128)(2,1)S(1)} %get-tuple-element.21), channel_id=1, source_target_pairs={{0,24},{8,32},{16,40},{24,48},{32,56},{40,64},{48,72},{56,80},{64,... | collective-permute-start | bytes 49160
  233.4 12.1 %collective-permute-start.16 = (bf16[64,128]{1,0:T(8,128)(2,1)S(1)}, bf16[64,128]{1,0:T(8,128)(2,1)S(1)}, u32[]{:S(2)}, u32[]{:S(2)}) collective-permute-start(bf16[64,128]{1,0:T(8,128)(2,1)S(1)} %get-tuple-element.21), channel_id=1, source_target_pairs={{0,32},{8,40},{16,48},{24,56},{32,64},{40,72},{48,80},{56,88},{64,... | collective-permute-start | bytes 49160
  237.4 51.3 %collective-permute-start.7 = (bf16[1,64,1,8,128]{4,1,3,2,0:T(8,128)(2,1)S(1)}, bf16[1,64,1,8,128]{4,1,3,2,0:T(8,128)(2,1)S(1)}, u32[]{:S(2)}, u32[]{:S(2)}) collective-permute-start(bf16[1,64,1,8,128]{4,1,3,2,0:T(8,128)(2,1)S(1)} %get-tuple-element.23), channel_id=1, source_target_pairs={{1,0},{2,1},{3,2},{4,3},{5,4},{6,5},{7,6},{9,8},{10,9},{11,10},{12... | collective-permute-start | bytes 393224 | tf_op jit(solution)/shard_map/ppermute | solution.py:15
  238.7 50.0 %collective-permute-start.6 = (bf16[1,64,1,8,128]{4,1,3,2,0:T(8,128)(2,1)S(1)}, bf16[1,64,1,8,128]{4,1,3,2,0:T(8,128)(2,1)S(1)}, u32[]{:S(2)}, u32[]{:S(2)}) collective-permute-start(bf16[1,64,1,8,128]{4,1,3,2,0:T(8,128)(2,1)S(1)} %get-tuple-element.22), channel_id=1, source_target_pairs={{0,1},{1,2},{2,3},{3,4},{4,5},{5,6},{6,7},{8,9},{9,10},{10,11},{11... | collective-permute-start | bytes 393224 | tf_op jit(solution)/shard_map/ppermute | solution.py:12
where the time goes:
time: 300 us; the launch traced here: 299 us
  blocking collectives  164 us (55%)
  starting transfers between devices  63.6 us (21%)
  matrix products  43 us (14%)
  other arithmetic  10.6 us (4%)
  local copies, waits for them, and re-layouts  9.04 us (3%)
  waiting for transfers between devices  5.7 us (2%)
  between operations  3.19 us (1%)
    unnamed x1, blocking collectives  53.5 us
    psum x1, blocking collectives, local(): lax.psum(rows_one.astype(jnp.bfloat16), 'space').astype(jnp.float32)  41 us
    all_gather x1, blocking collectives, local(): lax.all_gather(w_second, 'dp', axis=0, tiled=True)  35.1 us
    all_gather x1, blocking collectives, local(): lax.all_gather(w_first, 'dp', axis=0, tiled=True)  34.2 us
    unnamed x10, starting transfers between devices  34 us
    ppermute x4, starting transfers between devices, with_halo(): lax.ppermute(lax.slice_in_dim(block, block.shape[dim] - width, None, axis...  24.5 us
    dot_general x54, matrix products, conv_forward(): jnp.einsum('sixyz,io->soxyz', window, kernel[along_x, along_y, along_z],...  16.1 us
    dot_general x54, matrix products, conv_weight_grad(): jnp.einsum('sixyz,soxyz->io', window, grads, preferred_element_type=jnp.f...  13.8 us
  transfers between devices with their start and end apart: 18, of which 1 were waited for; matrix products, arithmetic and copies ran while one was open for 2% of the time, Pallas kernels for 0%

commit v1 on v0

v1 whole, which is shorter than its diff:
```python
import functools

import jax
import jax.numpy as jnp
from jax import lax
from jax.experimental import pallas as pl
from jax.experimental.pallas import tpu as pltpu
from jax.sharding import PartitionSpec as P

MESH = pl.DeviceIdType.MESH
F32 = jnp.float32
BF16 = jnp.bfloat16

DP = 32
SP = 8
CHIPS = 16
C0, C1, C2 = 32, 64, 128
X, Y, Z = 4, 8, 128
R1, R2 = 27, 54
FACTOR_ONE = float(1048576) ** (-0.5)
FACTOR_TWO = float(131072) ** (-0.5)


def dot(a, b):
    return lax.dot_general(a, b, (((1,), (0,)), ((), ())), preferred_element_type=F32)


def dot_nt(a, b):
    return lax.dot_general(a, b, (((1,), (1,)), ((), ())), preferred_element_type=F32)


def lanes(rows):
    return lax.broadcasted_iota(jnp.int32, (rows, Z), 1)


def shifted(tile, by):
    moved = pltpu.roll(tile, by % Z, 1)
    at = lanes(tile.shape[0])
    keep = at >= by if by > 0 else at < Z + by
    return jnp.where(keep, moved, 0.0)


def frame_plane(source, dest, rows, count, step):
    zero = jnp.zeros((3 * rows, Z), BF16)
    dest[0 : 3 * rows, 0:Z] = zero
    dest[6 * rows : 9 * rows, (count - 1) * Z : count * Z] = zero
    for y in range(count):
        tile = source[y]
        wide = tile.astype(F32)
        three = (shifted(wide, step).astype(BF16), tile, shifted(wide, -step).astype(BF16))
        for b in range(3):
            to = y - b + 1
            if 0 <= to < count:
                for c in range(3):
                    row = (b * 3 + c) * rows
                    dest[row : row + rows, to * Z : (to + 1) * Z] = three[c]


def gather_taps(parts, rows, count, y, step):
    total = None
    for c in range(3):
        column = None
        for b in range(3):
            at = y - b + 1
            if 0 <= at < count:
                row = (b * 3 + c) * rows
                piece = parts[row : row + rows, at * Z : (at + 1) * Z]
                column = piece if column is None else column + piece
        if c == 0:
            column = shifted(column, -step)
        elif c == 2:
            column = shifted(column, step)
        total = column if total is None else total + column
    return total


def kernel(
    vol, wpack, cot,
    pooled_out, vgrad_out, gone_out, gtwo_out,
    vp, s1, pre1, slope1, pp, s2, d2, d1, taps1, taps2,
    wg1, wg2, wf1, wf2, w1, w2, w1t, w2t,
    gs1, gs2, gp1, gp2, ra2, pb2, rb2, rb1, sc, rc,
    vin_sem, halo_send, halo_recv, w1_send, w1_recv, w2_send, w2_recv, wf_send, wf_recv,
    a2_send, a2_recv, b2_send, b2_recv, b1_send, b1_recv, c_send, c_recv,
):
    d = lax.axis_index("dp")
    s = lax.axis_index("space")
    core = lax.rem(d, 2)
    chip = d // 2
    sibling = chip * 2 + 1 - core

    def remote(src, dst, ssem, rsem, **where):
        return pltpu.make_async_remote_copy(
            src_ref=src, dst_ref=dst, send_sem=ssem, recv_sem=rsem,
            device_id=where, device_id_type=MESH,
        )

    barrier = pltpu.get_barrier_semaphore()

    def greet_dp(k, carry):
        pl.semaphore_signal(barrier, inc=1, device_id={"dp": lax.rem(d + k, DP)}, device_id_type=MESH)
        return carry

    def greet_space(k, carry):
        pl.semaphore_signal(barrier, inc=1, device_id={"space": lax.rem(s + k, SP)}, device_id_type=MESH)
        return carry

    vin = pltpu.make_async_copy(vol, vp.at[pl.ds(1, X)], vin_sem)
    vin.start()
    lax.fori_loop(1, DP, greet_dp, 0)
    lax.fori_loop(1, SP, greet_space, 0)
    pl.semaphore_wait(barrier, DP + SP - 2)

    def halo(n, low_src, high_src, low_dst, high_dst):
        up = remote(high_src, low_dst, halo_send.at[n, 0], halo_recv.at[n, 0], space=lax.rem(s + 1, SP))
        down = remote(low_src, high_dst, halo_send.at[n, 1], halo_recv.at[n, 1], space=lax.rem(s + SP - 1, SP))

        def start():
            @pl.when(s < SP - 1)
            def _():
                up.start()

            @pl.when(s > 0)
            def _():
                down.start()

        def wait():
            @pl.when(s > 0)
            def _():
                up.wait_recv()

            @pl.when(s == 0)
            def _():
                low_dst[...] = jnp.zeros(low_dst.shape, BF16)

            @pl.when(s < SP - 1)
            def _():
                down.wait_recv()

            @pl.when(s == SP - 1)
            def _():
                high_dst[...] = jnp.zeros(high_dst.shape, BF16)

        def drain():
            @pl.when(s < SP - 1)
            def _():
                up.wait_send()

            @pl.when(s > 0)
            def _():
                down.wait_send()

        return start, wait, drain

    def w1_copy(k):
        return remote(
            wpack.at[pl.ds(0, 16)], wg1.at[d], w1_send.at[k], w1_recv.at[k], dp=lax.rem(d + k, DP)
        )

    def w2_copy(k):
        peer = lax.rem(chip + k, CHIPS)
        return remote(
            wpack.at[pl.ds(16, 64)], wg2.at[chip, core], w2_send.at[k], w2_recv.at[k], dp=peer * 2 + core
        )

    def each(low, high, action):
        def body(k, carry):
            action(k)
            return carry

        lax.fori_loop(low, high, body, 0)

    each(1, DP, lambda k: w1_copy(k).start())
    v_start, v_wait, v_drain = halo(0, vol.at[0], vol.at[X - 1], vp.at[0], vp.at[X + 1])
    v_start()
    each(1, CHIPS, lambda k: w2_copy(k).start())
    wg1[d] = wpack[0:16]
    wg2[chip, core] = wpack[16:80]

    vin.wait()
    each(1, X + 1, lambda k: frame_plane(vp.at[k], s1.at[k], C0, Y, 1))
    v_wait()
    frame_plane(vp.at[0], s1.at[0], C0, Y, 1)
    frame_plane(vp.at[X + 1], s1.at[X + 1], C0, Y, 1)

    each(1, DP, lambda k: w1_copy(k).wait_recv())
    for k in range(DP):
        block = wg1[k].astype(F32)
        wf1[R1 * k : R1 * k + 16, 0:C1] = block[:, 0:C1]
        wf1[R1 * k + 16 : R1 * k + R1, 0:C1] = pltpu.roll(block, 64, 1)[0 : R1 - 16, 0:C1]
    w1[...] = wf1[...].astype(BF16)
    w1t[...] = wf1[...].T.astype(BF16)

    def first_layer(h):
        for k in range(2):
            x = 2 * h + k
            pre1[k] = dot(w1t[...], s1[pl.ds(x, 3)].reshape(27 * C0, Y * Z))
        even = lax.rem(lanes(C1), 2) == 0
        for y in range(Y // 2):
            total = jnp.zeros((C1, Z), F32)
            for k in range(2):
                for j in range(2):
                    at = slice((2 * y + j) * Z, (2 * y + j + 1) * Z)
                    t = pre1[k, :, at]
                    sigma = jax.nn.sigmoid(t)
                    total = total + t * sigma
                    slope1[2 * h + k, :, at] = sigma * (1.0 + t * (1.0 - sigma)) * 0.125
            other = jnp.where(even, pltpu.roll(total, Z - 1, 1), pltpu.roll(total, 1, 1))
            pp[h + 1, y] = ((total + other) * 0.125).astype(BF16)

    each(0, 2, first_layer)
    p_start, p_wait, p_drain = halo(1, pp.at[1], pp.at[2], pp.at[0], pp.at[3])
    p_start()

    each(1, CHIPS, lambda k: w2_copy(k).wait_recv())
    forward = remote(wg2.at[:, core], wg2.at[:, core], wf_send, wf_recv, dp=sibling)
    forward.start()
    each(1, 3, lambda k: frame_plane(pp.at[k], s2.at[k], C1, Y // 2, 2))
    forward.wait_recv()
    for k in range(DP):
        wf2[R2 * k : R2 * k + R2, :] = wg2[k // 2, k % 2].astype(F32)[0:R2]
    w2[...] = wf2[...].astype(BF16)
    w2t[...] = wf2[...].T.astype(BF16)
    p_wait()
    frame_plane(pp.at[0], s2.at[0], C1, Y // 2, 2)
    frame_plane(pp.at[3], s2.at[3], C1, Y // 2, 2)

    spread = jnp.where(
        lax.broadcasted_iota(jnp.int32, (32, Z), 1) // 4 == lax.broadcasted_iota(jnp.int32, (32, Z), 0), 1.0, 0.0
    ).astype(BF16)
    squeeze = jnp.where(
        lax.broadcasted_iota(jnp.int32, (Z, 32), 0) // 4 == lax.broadcasted_iota(jnp.int32, (Z, 32), 1), 0.5, 0.0
    ).astype(BF16)
    for x in range(2):
        taps2[0:C2, x * 512 : (x + 1) * 512] = dot(w2t[...], s2[x : x + 3].reshape(27 * C1, Y // 2 * Z))
    for y in range(2):
        spreaded = dot(cot[y], spread) * 0.125
        total = jnp.zeros((C2, Z), F32)
        for x in range(2):
            for j in range(2):
                yy = 2 * y + j
                t = taps2[0:C2, x * 512 + yy * Z : x * 512 + (yy + 1) * Z]
                sigma = jax.nn.sigmoid(t)
                total = total + t * sigma
                d2[x + 1, :, yy * Z : (yy + 1) * Z] = (
                    spreaded * (sigma * (1.0 + t * (1.0 - sigma)))
                ).astype(BF16)
        total = total * 0.125
        high = total.astype(BF16)
        low = (total - high.astype(F32)).astype(BF16)
        pooled_out[y] = (dot(high, squeeze) + dot(low, squeeze)).astype(BF16)
    e_start, e_wait, e_drain = halo(2, d2.at[1], d2.at[2], d2.at[0], d2.at[3])
    e_start()

    for a in range(3):
        gs2[a * 576 : (a + 1) * 576, :] = (
            dot_nt(s2[a], d2[1]) + dot_nt(s2[a + 1], d2[2])
        )
    for k in range(DP):
        gp2[k // 2, k % 2, 0:R2, :] = gs2[R2 * k : R2 * k + R2, :].astype(BF16)
        gp2[k // 2, k % 2, R2:64, :] = jnp.zeros((64 - R2, C2), BF16)
    pair = remote(gp2.at[:, 1 - core], ra2, a2_send, a2_recv, dp=sibling)
    pair.start()

    e_wait()
    left2 = jnp.concatenate([w2[1152:1728], w2[576:1152], w2[0:576]], axis=1)
    for x in range(2):
        taps2[:, 0:512] = dot(left2, d2[x : x + 3].reshape(3 * C2, 512))
        for y in range(Y // 2):
            grad = gather_taps(taps2, C1, Y // 2, y, 2).astype(BF16).astype(F32)
            for k in range(2):
                for j in range(2):
                    at = slice((2 * y + j) * Z, (2 * y + j + 1) * Z)
                    d1[2 * x + k + 1, :, at] = (grad * slope1[2 * x + k, :, at]).astype(BF16)
    f_start, f_wait, f_drain = halo(3, d1.at[1], d1.at[X], d1.at[0], d1.at[X + 1])
    f_start()

    pair.wait_recv()

    def add_pair(k):
        pb2[k] = (gp2[k, core].astype(F32) + ra2[k].astype(F32)).astype(BF16)

    each(0, CHIPS, add_pair)

    def b2_copy(k):
        peer = lax.rem(chip + k, CHIPS)
        return remote(pb2.at[peer], rb2.at[k], b2_send.at[k], b2_recv.at[k], dp=peer * 2 + core)

    each(1, CHIPS, lambda k: b2_copy(k).start())

    for a in range(3):
        acc = dot_nt(s1[a], d1[1])
        for x in range(1, X):
            acc = acc + dot_nt(s1[a + x], d1[x + 1])
        gs1[a * 288 : (a + 1) * 288, :] = acc
    for k in range(DP):
        head = gs1[R1 * k : R1 * k + 16, :].astype(BF16)
        tail = jnp.concatenate(
            [gs1[R1 * k + 16 : R1 * k + R1, :], jnp.zeros((32 - R1, C1), F32)], axis=0
        ).astype(BF16)
        gp1[k] = jnp.concatenate([head, tail], axis=1)

    def b1_copy(k):
        peer = lax.rem(d + k, DP)
        return remote(gp1.at[peer], rb1.at[k], b1_send.at[k], b1_recv.at[k], dp=peer)

    each(1, DP, lambda k: b1_copy(k).start())

    f_wait()
    left1 = jnp.concatenate([w1[576:864], w1[288:576], w1[0:288]], axis=1)

    def volume_grad(x):
        taps1[...] = dot(left1, d1[pl.ds(x, 3)].reshape(3 * C1, Y * Z))
        for y in range(Y):
            vgrad_out[x, y] = gather_taps(taps1, C0, Y, y, 1).astype(BF16)

    each(0, X, volume_grad)

    each(1, CHIPS, lambda k: b2_copy(k).wait_recv())
    sum2 = lax.fori_loop(1, CHIPS, lambda k, t: t + rb2[k].astype(F32), pb2[chip].astype(F32))
    sc[16:80] = sum2.astype(BF16)
    each(1, DP, lambda k: b1_copy(k).wait_recv())
    sum1 = lax.fori_loop(1, DP, lambda k, t: t + rb1[k].astype(F32), gp1[d].astype(F32))
    sc[0:16] = sum1.astype(BF16)

    def c_copy(k):
        return remote(sc, rc.at[k], c_send.at[k], c_recv.at[k], space=lax.rem(s + k, SP))

    each(1, SP, lambda k: c_copy(k).start())
    each(1, SP, lambda k: c_copy(k).wait_recv())
    full = lax.fori_loop(1, SP, lambda k, t: t + rc[k].astype(F32), sc[...].astype(F32))
    gtwo_out[...] = full[16 : 16 + R2] * (0.5 * FACTOR_TWO)
    gone_out[0:16, :] = full[0:16, 0:C1] * FACTOR_ONE
    gone_out[16:R1, :] = pltpu.roll(full[0:16], 64, 1)[0 : R1 - 16, 0:C1] * FACTOR_ONE

    v_drain()
    p_drain()
    e_drain()
    f_drain()
    each(1, DP, lambda k: w1_copy(k).wait_send())
    each(1, CHIPS, lambda k: w2_copy(k).wait_send())
    forward.wait_send()
    pair.wait_send()
    each(1, CHIPS, lambda k: b2_copy(k).wait_send())
    each(1, DP, lambda k: b1_copy(k).wait_send())
    each(1, SP, lambda k: c_copy(k).wait_send())


def local(volumes, w_first, w_second, cotangent):
    vol = volumes[0].transpose(1, 2, 0, 3)
    head = jnp.concatenate([w_first[0:16], jnp.pad(w_first[16:R1], ((0, 32 - R1), (0, 0)))], axis=1)
    wpack = jnp.concatenate([head, jnp.pad(w_second, ((0, 64 - R2), (0, 0)))], axis=0)
    cot = cotangent[0, :, 0].transpose(1, 0, 2)
    vmem = pl.BlockSpec(memory_space=pltpu.VMEM)
    dma = pltpu.SemaphoreType.DMA
    pooled, vgrad, gone, gtwo = pl.pallas_call(
        kernel,
        out_shape=(
            jax.ShapeDtypeStruct((2, C2, 32), BF16),
            jax.ShapeDtypeStruct((X, Y, C0, Z), BF16),
            jax.ShapeDtypeStruct((R1, C1), F32),
            jax.ShapeDtypeStruct((R2, C2), F32),
        ),
        in_specs=[pl.BlockSpec(memory_space=pl.ANY), vmem, vmem],
        out_specs=(vmem, vmem, vmem, vmem),
        scratch_shapes=[
            pltpu.VMEM((X + 2, Y, C0, Z), BF16),
            pltpu.VMEM((X + 2, 9 * C0, Y * Z), BF16),
            pltpu.VMEM((2, C1, Y * Z), F32),
            pltpu.VMEM((X, C1, Y * Z), F32),
            pltpu.VMEM((4, Y // 2, C1, Z), BF16),
            pltpu.VMEM((4, 9 * C1, Y // 2 * Z), BF16),
            pltpu.VMEM((4, C2, Y // 2 * Z), BF16),
            pltpu.VMEM((X + 2, C1, Y * Z), BF16),
            pltpu.VMEM((9 * C0, Y * Z), F32),
            pltpu.VMEM((9 * C1, Y * Z), F32),
            pltpu.VMEM((DP, 16, 128), BF16),
            pltpu.VMEM((CHIPS, 2, 64, 128), BF16),
            pltpu.VMEM((27 * C0, C1), F32),
            pltpu.VMEM((27 * C1, C2), F32),
            pltpu.VMEM((27 * C0, C1), BF16),
            pltpu.VMEM((27 * C1, C2), BF16),
            pltpu.VMEM((C1, 27 * C0), BF16),
            pltpu.VMEM((C2, 27 * C1), BF16),
            pltpu.VMEM((27 * C0, C1), F32),
            pltpu.VMEM((27 * C1, C2), F32),
            pltpu.VMEM((DP, 16, 128), BF16),
            pltpu.VMEM((CHIPS, 2, 64, 128), BF16),
            pltpu.VMEM((CHIPS, 64, 128), BF16),
            pltpu.VMEM((CHIPS, 64, 128), BF16),
            pltpu.VMEM((CHIPS, 64, 128), BF16),
            pltpu.VMEM((DP, 16, 128), BF16),
            pltpu.VMEM((80, 128), BF16),
            pltpu.VMEM((SP, 80, 128), BF16),
            dma,
            dma((4, 2)), dma((4, 2)),
            dma((DP,)), dma((DP,)),
            dma((CHIPS,)), dma((CHIPS,)),
            dma, dma,
            dma, dma,
            dma((CHIPS,)), dma((CHIPS,)),
            dma((DP,)), dma((DP,)),
            dma((SP,)), dma((SP,)),
        ],
        compiler_params=pltpu.CompilerParams(
            collective_id=0, has_side_effects=True, vmem_limit_bytes=48 * 1024 * 1024
        ),
    )(vol, wpack, cot)
    return (
        pooled.transpose(1, 0, 2)[None, :, None],
        vgrad.transpose(2, 0, 1, 3)[None],
        gone,
        gtwo,
    )


def solution(mesh):
    return jax.shard_map(
        local,
        mesh=mesh,
        in_specs=(
            P("dp", None, "space", None, None),
            P("dp", None),
            P("dp", None),
            P("dp", None, "space", None, None),
        ),
        out_specs=(
            P("dp", None, "space", None, None),
            P("dp", None, "space", None, None),
            P("dp", None),
            P("dp", None),
        ),
        check_vma=False,
    )
```

time: 300 us -> 62.7 us (0.21)
  the two profiles are of different devices: /device:TPU:32 before, /device:TPU:1 now
where the time goes in v1:
time: 62.7 us; the launch traced here: 62.3 us
  Pallas kernels  56.2 us (90%)
  local copies, waits for them, and re-layouts  4.59 us (7%)
  other arithmetic  0.8 us (1%)
  between operations  0.66 us (1%)
    pallas_call x1, Pallas kernels, local(): pl.pallas_call(kernel, out_shape=(jax.ShapeDtypeStruct((2, C2, 32), BF16)...  56.2 us
    unnamed x8, local copies, waits for them, and re-layouts  3.9 us

profile of v1, /device:TPU:1, one launch (start us, length us, event | category | flops | bytes accessed | tf_op | source)
XLA Modules:
  0.0 62.3 jit_solution(16365903803994947224)
XLA Ops:
  0.6 0.0 slice-start
  0.6 0.0 slice-start.1
  0.7 0.7 %slice-done = bf16[11,64]{1,0:T(8,128)(2,1)S(1)} async-done(((bf16[27,64]{1,0:T(8,128)(2,1)}), bf16[11,64]{1,0:T(8,128)(2,1)S(1)}, s32[]{:S(2)}) %slice-start) | async-done | bytes 1432 | tf_op jit(solution)/shard_map/slice | solution.py:351
  1.3 0.0 slice-done.1
  1.3 0.0 copy-start
  1.3 0.8 %fusion.4.wpack = bf16[80,128]{1,0:T(8,128)(2,1)S(1)} fusion(bf16[54,128]{1,0:T(8,128)(2,1)} %param.6, bf16[11,64]{1,0:T(8,128)(2,1)S(1)} %slice-done, bf16[16,64]{1,0:T(8,128)(2,1)S(1)} %slice-done.1), kind=kLoop, calls=%fused_computation.8 | loop fusion | flops 133120 | bytes 37760 | tf_op jit(solution)/shard_map/concatenate | solution.py:352
  2.1 0.0 copy-done
  2.1 0.1 copy.9
  2.3 1.1 %copy.13 = bf16[1,32,4,8,128]{4,1,3,2,0:T(8,128)(2,1)S(1)} copy(bf16[1,32,4,8,128]{4,3,2,1,0:T(8,128)(2,1)} %param.4) | data formatting | bytes 524288 | tf_op args[0]
  3.3 56.2 %shard_map.75 = (bf16[2,128,32]{2,1,0:T(8,128)(2,1)S(1)}, bf16[4,8,32,128]{3,2,1,0:T(8,128)(2,1)S(1)}, f32[27,64]{1,0:T(8,128)S(1)}, f32[54,128]{1,0:T(8,128)S(1)}) custom-call(bf16[4,8,32,128]{3,2,1,0:T(8,128)(2,1)S(1)} %bitcast.14, bf16[80,128]{1,0:T(8,128)(2,1)S(1)} %fusion.4.wpack, bf16[2,128,32]{2,1,0:T(8,128)(2,1)S(1)} %bitcast.16), custom_call_target="tpu_custom_call" | custom-call | tf_op jit(solution)/shard_map/pallas_call | solution.py:356
  59.6 0.7 %copy.10 = bf16[1,128,1,2,32]{1,4,3,2,0:T(8,128)(2,1)} copy(bf16[1,128,1,2,32]{4,1,3,2,0:T(8,128)(2,1)S(1)} %bitcast.17) | data formatting | bytes 32768
  60.2 0.8 %copy.11 = bf16[1,32,4,8,128]{4,3,2,1,0:T(8,128)(2,1)} copy(bf16[1,32,4,8,128]{4,1,3,2,0:T(8,128)(2,1)S(1)} %bitcast.15) | data formatting | bytes 524288
  61.1 0.6 copy.16
  61.7 0.6 copy.17
Async XLA Ops:
  0.6 0.7 %slice-start = ((bf16[27,64]{1,0:T(8,128)(2,1)}), bf16[11,64]{1,0:T(8,128)(2,1)S(1)}, s32[]{:S(2)}) async-start(bf16[27,64]{1,0:T(8,128)(2,1)} %param.5), calls=%async_computation | async-start | bytes 8192 | tf_op jit(solution)/shard_map/slice | solution.py:351
  0.6 0.7 %slice-start.1 = ((bf16[27,64]{1,0:T(8,128)(2,1)}), bf16[16,64]{1,0:T(8,128)(2,1)S(1)}, s32[]{:S(2)}) async-start(bf16[27,64]{1,0:T(8,128)(2,1)} %param.5), calls=%async_computation.1 | async-start | bytes 8192 | tf_op jit(solution)/shard_map/slice | solution.py:351
  1.3 0.8 %copy-start = (bf16[1,128,1,2,32]{1,4,3,2,0:T(8,128)(2,1)S(1)}, bf16[1,128,1,2,32]{1,4,3,2,0:T(8,128)(2,1)}, u32[]{:S(2)}) copy-start(bf16[1,128,1,2,32]{1,4,3,2,0:T(8,128)(2,1)} %param.7) | copy-start | bytes 49156

commit v2 on v1

v2 whole, which is shorter than its diff:
```python
import functools

import jax
import jax.numpy as jnp
from jax import lax
from jax.experimental import pallas as pl
from jax.experimental.pallas import tpu as pltpu
from jax.sharding import PartitionSpec as P

MESH = pl.DeviceIdType.MESH
F32 = jnp.float32
BF16 = jnp.bfloat16

DP = 32
SP = 8
CHIPS = 16
C0, C1, C2 = 32, 64, 128
X, Y, Z = 4, 8, 128
R1, R2 = 27, 54
VMEM_BYTES = 56 * 1024 * 1024
FACTOR_ONE = float(1048576) ** (-0.5)
FACTOR_TWO = float(131072) ** (-0.5)


def dot(a, b):
    return lax.dot_general(a, b, (((1,), (0,)), ((), ())), preferred_element_type=F32)


def dot_nt(a, b):
    return lax.dot_general(a, b, (((1,), (1,)), ((), ())), preferred_element_type=F32)


def lanes(rows):
    return lax.broadcasted_iota(jnp.int32, (rows, Z), 1)


def shifted(tile, by):
    moved = pltpu.roll(tile, by % Z, 1)
    at = lanes(tile.shape[0])
    keep = at >= by if by > 0 else at < Z + by
    return jnp.where(keep, moved, 0.0)


def frame_plane(source, dest, rows, count, step):
    zero = jnp.zeros((3 * rows, Z), BF16)
    dest[0 : 3 * rows, 0:Z] = zero
    dest[6 * rows : 9 * rows, (count - 1) * Z : count * Z] = zero
    for y in range(count):
        wide = source(y)
        three = [t.astype(BF16) for t in (shifted(wide, step), wide, shifted(wide, -step))]
        for b in range(3):
            to = y - b + 1
            if 0 <= to < count:
                for c in range(3):
                    row = (b * 3 + c) * rows
                    dest[row : row + rows, to * Z : (to + 1) * Z] = three[c]


def gather_taps(parts, rows, count, y, step):
    total = None
    for c in range(3):
        column = None
        for b in range(3):
            at = y - b + 1
            if 0 <= at < count:
                row = (b * 3 + c) * rows
                piece = parts[row : row + rows, at * Z : (at + 1) * Z]
                column = piece if column is None else column + piece
        if c == 0:
            column = shifted(column, -step)
        elif c == 2:
            column = shifted(column, step)
        total = column if total is None else total + column
    return total


def kernel(
    vol_in, wone_in, wtwo_in, cot_in,
    pooled_to, vgrad_to, gone_to, gtwo_to,
    pooled_out, vgrad_out, gone_out, gtwo_out, vol, wone, wtwo, cot, vh, fst, s1, pre1, slope1, pp, ps, ph, s2, pre2, d2, es, eh, d1, taps1, taps2, fs, fh,
    wpad, wsend, wg1, wg2, wf1, wf2, w1, w2, w1t, w2t,
    gs1, gs2, gp1, gp2, ra1, ra2, pb1, pb2, rb1, rb2, sc1, sc2, rc1, rc2,
    in_sem, out_sem, halo_send, halo_recv, pair_send, pair_recv,
    w1_send, w1_recv, w2_send, w2_recv,
    b1_send, b1_recv, b2_send, b2_recv, c1_send, c1_recv, c2_send, c2_recv,
):
    d = lax.axis_index("dp")
    s = lax.axis_index("space")
    core = lax.rem(d, 2)
    chip = d // 2
    sibling = chip * 2 + 1 - core

    def remote(src, dst, ssem, rsem, **where):
        return pltpu.make_async_remote_copy(
            src_ref=src, dst_ref=dst, send_sem=ssem, recv_sem=rsem,
            device_id=where, device_id_type=MESH,
        )

    def each(low, high, action):
        def body(k, carry):
            action(k)
            return carry

        lax.fori_loop(low, high, body, 0)

    def peer(k):
        return lax.rem(chip + k, CHIPS) * 2 + core

    def greet(**where):
        pl.semaphore_signal(barrier, inc=1, device_id=where, device_id_type=MESH)

    barrier = pltpu.get_barrier_semaphore()
    loads = [
        pltpu.make_async_copy(src, dst, in_sem.at[k])
        for k, (src, dst) in enumerate(((wone_in, wone), (wtwo_in, wtwo), (vol_in, vol), (cot_in, cot)))
    ]
    for load in loads:
        load.start()
    each(1, CHIPS, lambda k: greet(dp=peer(k)))
    each(1, SP, lambda k: greet(space=lax.rem(s + k, SP)))
    greet(dp=sibling)

    loads[0].wait()
    loads[1].wait()
    wpad[0:R1] = wone[...].astype(F32)
    wpad[R1:32] = jnp.zeros((32 - R1, C1), F32)
    wsend[0:16] = jnp.concatenate([wpad[0:16], wpad[16:32]], axis=1).astype(BF16)
    wsend[16 : 16 + R2] = wtwo[...]
    wsend[16 + R2 : 80] = jnp.zeros((64 - R2, C2), BF16)
    wg1[chip, core] = wsend[0:16]
    wg2[chip, core] = wsend[16:80]
    loads[2].wait()
    for k in range(2):
        vh[k] = vol[0, :, 0 if k == 0 else X - 1]
    pl.semaphore_wait(barrier, CHIPS - 1 + SP - 1 + 1)

    def halo(n, low_src, high_src, low_dst, high_dst):
        up = remote(high_src, low_dst, halo_send.at[n, 0], halo_recv.at[n, 0], space=lax.rem(s + 1, SP))
        down = remote(low_src, high_dst, halo_send.at[n, 1], halo_recv.at[n, 1], space=lax.rem(s + SP - 1, SP))

        def start():
            @pl.when(s < SP - 1)
            def _():
                up.start()

            @pl.when(s > 0)
            def _():
                down.start()

        def wait():
            @pl.when(s > 0)
            def _():
                up.wait_recv()

            @pl.when(s == 0)
            def _():
                low_dst[...] = jnp.zeros(low_dst.shape, BF16)

            @pl.when(s < SP - 1)
            def _():
                down.wait_recv()

            @pl.when(s == SP - 1)
            def _():
                high_dst[...] = jnp.zeros(high_dst.shape, BF16)

        def drain():
            @pl.when(s < SP - 1)
            def _():
                up.wait_send()

            @pl.when(s > 0)
            def _():
                down.wait_send()

        return start, wait, drain

    def w1_copy(k):
        return remote(wsend.at[pl.ds(0, 16)], wg1.at[chip, core], w1_send.at[k], w1_recv.at[k], dp=peer(k))

    def w2_copy(k):
        return remote(wsend.at[pl.ds(16, 64)], wg2.at[chip, core], w2_send.at[k], w2_recv.at[k], dp=peer(k))

    each(1, CHIPS, lambda k: w1_copy(k).start())
    v_start, v_wait, v_drain = halo(0, vh.at[0], vh.at[1], vh.at[2], vh.at[3])
    v_start()
    each(1, CHIPS, lambda k: w2_copy(k).start())

    def frame_input(plane, dest):
        fst[...] = plane.astype(F32).reshape(C0 * Y, Z)
        frame_plane(lambda y: fst[pl.ds(y, C0, stride=Y), :], dest, C0, Y, 1)

    each(0, X, lambda k: frame_input(vol[0, :, k], s1.at[k + 1]))

    each(1, CHIPS, lambda k: w1_copy(k).wait_recv())
    forward1 = remote(wg1.at[:, core], wg1.at[:, core], pair_send.at[0], pair_recv.at[0], dp=sibling)
    forward1.start()
    v_wait()
    each(0, 2, lambda k: frame_input(vh[k + 2], s1.at[k * (X + 1)]))
    forward1.wait_recv()
    for k in range(DP):
        block = wg1[k // 2, k % 2].astype(F32)
        wf1[R1 * k : R1 * k + 16, 0:C1] = block[:, 0:C1]
        wf1[R1 * k + 16 : R1 * k + R1, 0:C1] = pltpu.roll(block, 64, 1)[0 : R1 - 16, 0:C1]
    w1[...] = wf1[...].astype(BF16)
    w1t[...] = wf1[...].T.astype(BF16)

    even = lax.rem(lanes(C1), 2) == 0

    def first_layer(h):
        for k in range(2):
            x = 2 * h + k
            pre1[k] = dot(w1t[...], s1[pl.ds(x, 3)].reshape(27 * C0, Y * Z))
        for y in range(Y // 2):
            total = jnp.zeros((C1, Z), F32)
            for k in range(2):
                for j in range(2):
                    at = slice((2 * y + j) * Z, (2 * y + j + 1) * Z)
                    t = pre1[k, :, at]
                    sigma = jax.nn.sigmoid(t)
                    total = total + t * sigma
                    slope1[2 * h + k, :, at] = sigma * (1.0 + t * (1.0 - sigma)) * 0.125
            other = jnp.where(even, pltpu.roll(total, Z - 1, 1), pltpu.roll(total, 1, 1))
            pp[h, y] = (total + other) * 0.125

    each(0, 2, first_layer)
    for h in range(2):
        for y in range(2):
            ps[h, y] = jnp.where(even, pp[h, 2 * y], pp[h, 2 * y + 1]).astype(BF16)
    p_start, p_wait, p_drain = halo(1, ps.at[0], ps.at[1], ph.at[0], ph.at[1])
    p_start()

    def apart(pairs, y):
        wide = pairs[y // 2].astype(F32)
        if y % 2 == 0:
            return jnp.where(even, wide, pltpu.roll(wide, 1, 1))
        return jnp.where(even, pltpu.roll(wide, Z - 1, 1), wide)

    each(1, CHIPS, lambda k: w2_copy(k).wait_recv())
    forward2 = remote(wg2.at[:, core], wg2.at[:, core], pair_send.at[1], pair_recv.at[1], dp=sibling)
    forward2.start()
    for h in range(2):
        frame_plane(lambda y: pp[h, y], s2.at[h + 1], C1, Y // 2, 2)
    forward2.wait_recv()
    for k in range(DP):
        wf2[R2 * k : R2 * k + R2, :] = wg2[k // 2, k % 2].astype(F32)[0:R2]
    w2[...] = wf2[...].astype(BF16)
    w2t[...] = wf2[...].T.astype(BF16)
    p_wait()
    for h in range(2):
        frame_plane(lambda y: apart(ph[h], y), s2.at[3 * h], C1, Y // 2, 2)

    loads[3].wait()
    spread = jnp.where(
        lax.broadcasted_iota(jnp.int32, (32, Z), 1) // 4 == lax.broadcasted_iota(jnp.int32, (32, Z), 0), 1.0, 0.0
    ).astype(BF16)
    squeeze = jnp.where(
        lax.broadcasted_iota(jnp.int32, (32, Z), 1) // 4 == lax.broadcasted_iota(jnp.int32, (32, Z), 0), 0.5, 0.0
    ).astype(BF16)
    for x in range(2):
        pre2[x] = dot(w2t[...], s2[x : x + 3].reshape(27 * C1, Y // 2 * Z))
    sums = []
    for y in range(2):
        spreaded = lax.dot_general(cot[y], spread, (((0,), (0,)), ((), ())), preferred_element_type=F32) * 0.125
        total = jnp.zeros((C2, Z), F32)
        for x in range(2):
            for j in range(2):
                at = slice((2 * y + j) * Z, (2 * y + j + 1) * Z)
                t = pre2[x, :, at]
                sigma = jax.nn.sigmoid(t)
                total = total + t * sigma
                d2[x, :, at] = (spreaded * (sigma * (1.0 + t * (1.0 - sigma)))).astype(BF16)
        sums.append(total)

    for k in range(2):
        taps2[0:576] = dot(w2[1152 * k : 1152 * k + 576], d2[k])
        for y in range(2):
            a, b = (gather_taps(taps2, C1, Y // 2, 2 * y + j, 2) for j in range(2))
            es[k, y] = jnp.where(even, a, b).astype(BF16)
    e_start, e_wait, e_drain = halo(2, es.at[0], es.at[1], eh.at[0], eh.at[1])
    e_start()

    for a in range(3):
        gs2[a * 576 : (a + 1) * 576, :] = dot_nt(s2[a], d2[0]) + dot_nt(s2[a + 1], d2[1])
    for k in range(DP):
        gp2[k // 2, k % 2, 0:R2, :] = gs2[R2 * k : R2 * k + R2, :].astype(BF16)
        gp2[k // 2, k % 2, R2:64, :] = jnp.zeros((64 - R2, C2), BF16)
    pair2 = remote(gp2.at[:, 1 - core], ra2, pair_send.at[2], pair_recv.at[2], dp=sibling)
    pair2.start()

    for x in range(2):
        left = jnp.concatenate([w2[(x + 1) * 576 : (x + 2) * 576], w2[x * 576 : (x + 1) * 576]], axis=1)
        taps2[x * 576 : (x + 1) * 576] = dot(left, d2[...].reshape(2 * C2, Y // 2 * Z))

    for y in range(2):
        total = sums[y] * 0.125
        high = total.astype(BF16)
        low = (total - high.astype(F32)).astype(BF16)
        pooled_out[y] = (dot_nt(squeeze, high) + dot_nt(squeeze, low)).astype(BF16)
    store_pooled = pltpu.make_async_copy(pooled_out, pooled_to, out_sem.at[X])
    store_pooled.start()

    pair2.wait_recv()

    def add_pair2(k):
        pb2[k] = (gp2[k, core].astype(F32) + ra2[k].astype(F32)).astype(BF16)

    each(0, CHIPS, add_pair2)

    def b2_copy(k):
        return remote(
            pb2.at[lax.rem(chip + k, CHIPS)], rb2.at[k], b2_send.at[k], b2_recv.at[k], dp=peer(k)
        )

    each(1, CHIPS, lambda k: b2_copy(k).start())

    e_wait()
    for k in range(2):
        d1[k] = jnp.zeros((C1, Y * Z), BF16)
        d1[X + 2 + k] = jnp.zeros((C1, Y * Z), BF16)
    for x in range(2):
        for y in range(Y // 2):
            grad = gather_taps(taps2.at[x * 576 : (x + 1) * 576], C1, Y // 2, y, 2) + apart(eh[x], y)
            grad = grad.astype(BF16).astype(F32)
            for k in range(2):
                for j in range(2):
                    at = slice((2 * y + j) * Z, (2 * y + j + 1) * Z)
                    d1[2 * x + k + 2, :, at] = (grad * slope1[2 * x + k, :, at]).astype(BF16)

    def add_plane(k, acc):
        return acc + dot_nt(s1[k], d1[pl.ds(k, 3)].reshape(3 * C1, Y * Z))

    acc = lax.fori_loop(0, X + 2, add_plane, jnp.zeros((9 * C0, 3 * C1), F32))
    for a in range(3):
        gs1[a * 288 : (a + 1) * 288, :] = acc[:, (2 - a) * C1 : (3 - a) * C1]
    for k in range(DP):
        head = gs1[R1 * k : R1 * k + 16, :].astype(BF16)
        tail = jnp.concatenate(
            [gs1[R1 * k + 16 : R1 * k + R1, :], jnp.zeros((32 - R1, C1), F32)], axis=0
        ).astype(BF16)
        gp1[k // 2, k % 2] = jnp.concatenate([head, tail], axis=1)
    pair1 = remote(gp1.at[:, 1 - core], ra1, pair_send.at[3], pair_recv.at[3], dp=sibling)
    pair1.start()

    for k in range(2):
        taps1[...] = dot(w1[576 * k : 576 * k + 288], d1[2 + (X - 1) * k])
        for y in range(Y):
            fs[k, y] = gather_taps(taps1, C0, Y, y, 1).astype(BF16)
    f_start, f_wait, f_drain = halo(3, fs.at[0], fs.at[1], fh.at[0], fh.at[1])
    f_start()

    pair1.wait_recv()

    def add_pair1(k):
        pb1[k] = (gp1[k, core].astype(F32) + ra1[k].astype(F32)).astype(BF16)

    each(0, CHIPS, add_pair1)

    def b1_copy(k):
        return remote(
            pb1.at[lax.rem(chip + k, CHIPS)], rb1.at[k], b1_send.at[k], b1_recv.at[k], dp=peer(k)
        )

    each(1, CHIPS, lambda k: b1_copy(k).start())

    left1 = jnp.concatenate([w1[576:864], w1[288:576], w1[0:288]], axis=1)

    def store_vgrad(x):
        return pltpu.make_async_copy(vgrad_out.at[x], vgrad_to.at[0, :, x], out_sem.at[x])

    def volume_grad(x, extra=None):
        taps1[...] = dot(left1, d1[pl.ds(x + 1, 3)].reshape(3 * C1, Y * Z))
        for y in range(Y):
            piece = gather_taps(taps1, C0, Y, y, 1)
            if extra is not None:
                piece = piece + extra[y].astype(F32)
            fst[pl.ds(y, C0, stride=Y), :] = piece
        vgrad_out[x] = fst[...].reshape(C0, Y, Z).astype(BF16)
        store_vgrad(x).start()

    each(1, X - 1, volume_grad)
    each(1, CHIPS, lambda k: b2_copy(k).wait_recv())
    sum2 = lax.fori_loop(1, CHIPS, lambda k, t: t + rb2[k].astype(F32), pb2[chip].astype(F32))
    sc2[...] = sum2.astype(BF16)

    def c2_copy(k):
        return remote(sc2, rc2.at[k], c2_send.at[k], c2_recv.at[k], space=lax.rem(s + k, SP))

    each(1, SP, lambda k: c2_copy(k).start())
    f_wait()
    each(0, 2, lambda k: volume_grad((X - 1) * k, fh.at[k]))

    each(1, CHIPS, lambda k: b1_copy(k).wait_recv())
    sum1 = lax.fori_loop(1, CHIPS, lambda k, t: t + rb1[k].astype(F32), pb1[chip].astype(F32))
    sc1[...] = sum1.astype(BF16)

    def c1_copy(k):
        return remote(sc1, rc1.at[k], c1_send.at[k], c1_recv.at[k], space=lax.rem(s + k, SP))

    each(1, SP, lambda k: c1_copy(k).start())
    each(1, SP, lambda k: c2_copy(k).wait_recv())
    full2 = lax.fori_loop(1, SP, lambda k, t: t + rc2[k].astype(F32), sc2[...].astype(F32))
    gtwo_out[...] = full2[0:R2] * (0.5 * FACTOR_TWO)
    store_gtwo = pltpu.make_async_copy(gtwo_out, gtwo_to, out_sem.at[X + 1])
    store_gtwo.start()

    v_drain()
    p_drain()
    e_drain()
    f_drain()
    each(1, CHIPS, lambda k: w1_copy(k).wait_send())
    each(1, CHIPS, lambda k: w2_copy(k).wait_send())
    each(1, CHIPS, lambda k: b2_copy(k).wait_send())
    each(1, CHIPS, lambda k: b1_copy(k).wait_send())
    forward1.wait_send()
    forward2.wait_send()
    pair1.wait_send()
    pair2.wait_send()
    each(1, SP, lambda k: c2_copy(k).wait_send())
    each(1, SP, lambda k: c1_copy(k).wait_send())

    each(1, SP, lambda k: c1_copy(k).wait_recv())
    full1 = lax.fori_loop(1, SP, lambda k, t: t + rc1[k].astype(F32), sc1[...].astype(F32))
    gone_out[0:16, :] = full1[:, 0:C1] * FACTOR_ONE
    gone_out[16:R1, :] = pltpu.roll(full1, 64, 1)[0 : R1 - 16, 0:C1] * FACTOR_ONE
    store_gone = pltpu.make_async_copy(gone_out, gone_to, out_sem.at[X + 2])
    store_gone.start()
    each(0, X, lambda k: store_vgrad(k).wait())
    store_pooled.wait()
    store_gtwo.wait()
    store_gone.wait()


def hand_over(*refs):
    sources, dests, held, sem = refs[0:4], refs[4:8], refs[8:12], refs[12]
    loads = [pltpu.make_async_copy(sources[k], held[k], sem.at[0, k]) for k in range(4)]
    stores = [pltpu.make_async_copy(held[k], dests[k], sem.at[1, k]) for k in range(4)]
    for load in loads:
        load.start()
    for load, store in zip(loads, stores):
        load.wait()
        store.start()
    for store in stores:
        store.wait()


def local(volumes, w_first, w_second, cotangent):
    cot = cotangent[0, :, 0].transpose(1, 2, 0)
    hbm = pl.BlockSpec(memory_space=pltpu.HBM)
    shapes = (
        jax.ShapeDtypeStruct((2, 32, C2), BF16),
        jax.ShapeDtypeStruct((1, C0, X, Y, Z), BF16),
        jax.ShapeDtypeStruct((R1, C1), F32),
        jax.ShapeDtypeStruct((R2, C2), F32),
    )
    dma = pltpu.SemaphoreType.DMA
    results = pl.pallas_call(
        kernel,
        out_shape=shapes,
        in_specs=[hbm] * 4,
        out_specs=(hbm,) * 4,
        scratch_shapes=[
            pltpu.VMEM((2, 32, C2), BF16),
            pltpu.VMEM((X, C0, Y, Z), BF16),
            pltpu.VMEM((R1, C1), F32),
            pltpu.VMEM((R2, C2), F32),
            pltpu.VMEM((1, C0, X, Y, Z), BF16),
            pltpu.VMEM((R1, C1), BF16),
            pltpu.VMEM((R2, C2), BF16),
            pltpu.VMEM((2, 32, C2), BF16),
            pltpu.VMEM((4, C0, Y, Z), BF16),
            pltpu.VMEM((C0 * Y, Z), F32),
            pltpu.VMEM((X + 2, 9 * C0, Y * Z), BF16),
            pltpu.VMEM((2, C1, Y * Z), F32),
            pltpu.VMEM((X, C1, Y * Z), F32),
            pltpu.VMEM((2, Y // 2, C1, Z), F32),
            pltpu.VMEM((2, 2, C1, Z), BF16),
            pltpu.VMEM((2, 2, C1, Z), BF16),
            pltpu.VMEM((4, 9 * C1, Y // 2 * Z), BF16),
            pltpu.VMEM((2, C2, Y // 2 * Z), F32),
            pltpu.VMEM((2, C2, Y // 2 * Z), BF16),
            pltpu.VMEM((2, 2, C1, Z), BF16),
            pltpu.VMEM((2, 2, C1, Z), BF16),
            pltpu.VMEM((X + 4, C1, Y * Z), BF16),
            pltpu.VMEM((9 * C0, Y * Z), F32),
            pltpu.VMEM((18 * C1, Y // 2 * Z), F32),
            pltpu.VMEM((2, Y, C0, Z), BF16),
            pltpu.VMEM((2, Y, C0, Z), BF16),
            pltpu.VMEM((32, C1), F32),
            pltpu.VMEM((80, 128), BF16),
            pltpu.VMEM((CHIPS, 2, 16, 128), BF16),
            pltpu.VMEM((CHIPS, 2, 64, 128), BF16),
            pltpu.VMEM((27 * C0, C1), F32),
            pltpu.VMEM((27 * C1, C2), F32),
            pltpu.VMEM((27 * C0, C1), BF16),
            pltpu.VMEM((27 * C1, C2), BF16),
            pltpu.VMEM((C1, 27 * C0), BF16),
            pltpu.VMEM((C2, 27 * C1), BF16),
            pltpu.VMEM((27 * C0, C1), F32),
            pltpu.VMEM((27 * C1, C2), F32),
            pltpu.VMEM((CHIPS, 2, 16, 128), BF16),
            pltpu.VMEM((CHIPS, 2, 64, 128), BF16),
            pltpu.VMEM((CHIPS, 16, 128), BF16),
            pltpu.VMEM((CHIPS, 64, 128), BF16),
            pltpu.VMEM((CHIPS, 16, 128), BF16),
            pltpu.VMEM((CHIPS, 64, 128), BF16),
            pltpu.VMEM((CHIPS, 16, 128), BF16),
            pltpu.VMEM((CHIPS, 64, 128), BF16),
            pltpu.VMEM((16, 128), BF16),
            pltpu.VMEM((64, 128), BF16),
            pltpu.VMEM((SP, 16, 128), BF16),
            pltpu.VMEM((SP, 64, 128), BF16),
            dma((4,)), dma((X + 3,)),
            dma((4, 2)), dma((4, 2)),
            dma((4,)), dma((4,)),
            dma((CHIPS,)), dma((CHIPS,)),
            dma((CHIPS,)), dma((CHIPS,)),
            dma((CHIPS,)), dma((CHIPS,)),
            dma((CHIPS,)), dma((CHIPS,)),
            dma((SP,)), dma((SP,)),
            dma((SP,)), dma((SP,)),
        ],
        compiler_params=pltpu.CompilerParams(
            collective_id=0, has_side_effects=True, vmem_limit_bytes=VMEM_BYTES
        ),
    )(volumes, w_first, w_second, cot)
    pooled, vgrad, gone, gtwo = pl.pallas_call(
        hand_over,
        out_shape=shapes,
        in_specs=[hbm] * 4,
        out_specs=(hbm,) * 4,
        scratch_shapes=[*(pltpu.VMEM(each.shape, each.dtype) for each in shapes), dma((2, 4))],
        compiler_params=pltpu.CompilerParams(vmem_limit_bytes=VMEM_BYTES),
    )(*results)
    return (pooled.transpose(2, 0, 1)[None, :, None], vgrad, gone, gtwo)


def solution(mesh):
    return jax.shard_map(
        local,
        mesh=mesh,
        in_specs=(
            P("dp", None, "space", None, None),
            P("dp", None),
            P("dp", None),
            P("dp", None, "space", None, None),
        ),
        out_specs=(
            P("dp", None, "space", None, None),
            P("dp", None, "space", None, None),
            P("dp", None),
            P("dp", None),
        ),
        check_vma=False,
    )
```

time: 62.7 us -> 49.8 us (0.79)
  Pallas kernels: 56.2 us -> 48.9 us
  local copies, waits for them, and re-layouts: 4.59 us -> 0 us
  other arithmetic: 0.8 us -> 0 us
    pallas_call x1 -> x2, Pallas kernels: 56.2 us -> 48.9 us  [the longest x1 47.2 us: local(): pl.pallas_call(kernel, out_shape=shapes, in_specs=[hbm] * 4, out_specs=(h...]
    unnamed x8 -> x0, local copies, waits for them, and re-layouts: 3.9 us -> none
    concatenate x1 -> x0, other arithmetic: 0.8 us -> none  [local(): jnp.concatenate([head, jnp.pad(w_second, ((0, 64 - R2), (0, 0)))], axis=0)]
    slice x4 -> x0, local copies, waits for them, and re-layouts: 0.69 us -> none  [the longest x2 0.67 us: local(): w_first[16:R1]]
where the time goes in v2:
time: 49.8 us; the launch traced here: 49.6 us
  Pallas kernels  48.9 us (98%)
  between operations  0.64 us (1%)
    pallas_call x1, Pallas kernels, local(): pl.pallas_call(kernel, out_shape=shapes, in_specs=[hbm] * 4, out_specs=(h...  47.2 us
    pallas_call x1, Pallas kernels, local(): pl.pallas_call(hand_over, out_shape=shapes, in_specs=[hbm] * 4, out_specs...  1.74 us

profile of v2, /device:TPU:1, one launch (start us, length us, event | category | flops | bytes accessed | tf_op | source)
XLA Modules:
  0.0 49.6 jit_solution(9946965704024648275)
XLA Ops:
  0.6 47.2 %shard_map.75 = (bf16[2,32,128]{2,1,0:T(8,128)(2,1)}, bf16[1,32,4,8,128]{4,3,2,1,0:T(8,128)(2,1)}, f32[27,64]{1,0:T(8,128)}, f32[54,128]{1,0:T(8,128)}) custom-call(bf16[1,32,4,8,128]{4,3,2,1,0:T(8,128)(2,1)} %vol_in.1, bf16[27,64]{1,0:T(8,128)(2,1)} %wone_in.1, bf16[54,128]{1,0:T(8,128)(2,1)} %wtwo_in.1, bf16[2,32,128]{2,1,0:T(8,128)(2,1)} %bitcast.6), custom_call_target="tpu_custom_call" | custom-call | tf_op jit(solution)/shard_map/pallas_call | solution.py:457
  47.8 1.7 %shard_map.76 = (bf16[2,32,128]{2,1,0:T(8,128)(2,1)}, bf16[1,32,4,8,128]{4,3,2,1,0:T(8,128)(2,1)}, f32[27,64]{1,0:T(8,128)}, f32[54,128]{1,0:T(8,128)}) custom-call(bf16[2,32,128]{2,1,0:T(8,128)(2,1)} %get-tuple-element.12.refs_0_, bf16[1,32,4,8,128]{4,3,2,1,0:T(8,128)(2,1)} %get-tuple-element.13.refs_1_, f32[27,64]{1,0:T(8,128)} %get-tuple-element.14.refs_2_, ...), custom_call_target="tpu_custom_call" | custom-call | tf_op jit(solution)/shard_map/pallas_call | solution.py:527

commit v3 on v2

--- a/solution.py
+++ b/solution.py
@@ -17,7 +17,7 @@
 C0, C1, C2 = 32, 64, 128
 X, Y, Z = 4, 8, 128
 R1, R2 = 27, 54
-VMEM_BYTES = 56 * 1024 * 1024
+VMEM_BYTES = 48 * 1024 * 1024
 FACTOR_ONE = float(1048576) ** (-0.5)
 FACTOR_TWO = float(131072) ** (-0.5)
 
@@ -76,11 +76,11 @@
 
 def kernel(
     vol_in, wone_in, wtwo_in, cot_in,
-    pooled_to, vgrad_to, gone_to, gtwo_to,
-    pooled_out, vgrad_out, gone_out, gtwo_out, vol, wone, wtwo, cot, vh, fst, s1, pre1, slope1, pp, ps, ph, s2, pre2, d2, es, eh, d1, taps1, taps2, fs, fh,
+    pooled_out, vgrad_out, gone_out, gtwo_out,
+    vol, wone, wtwo, cot, vh, fst, s1, pre1, slope1, pp, ps, ph, s2, pre2, d2, es, eh, d1, taps1, grow, taps2, edge2, fs, fh,
     wpad, wsend, wg1, wg2, wf1, wf2, w1, w2, w1t, w2t,
     gs1, gs2, gp1, gp2, ra1, ra2, pb1, pb2, rb1, rb2, sc1, sc2, rc1, rc2,
-    in_sem, out_sem, halo_send, halo_recv, pair_send, pair_recv,
+    in_sem, halo_send, halo_recv, pair_send, pair_recv,
     w1_send, w1_recv, w2_send, w2_recv,
     b1_send, b1_recv, b2_send, b2_recv, c1_send, c1_recv, c2_send, c2_recv,
 ):
@@ -95,6 +95,9 @@
             src_ref=src, dst_ref=dst, send_sem=ssem, recv_sem=rsem,
             device_id=where, device_id_type=MESH,
         )
+
+    def whole(view, ssem, rsem):
+        return remote(view, view, ssem, rsem, dp=sibling)
 
     def each(low, high, action):
         def body(k, carry):
@@ -176,11 +179,17 @@
         return start, wait, drain
 
     def w1_copy(k):
-        return remote(wsend.at[pl.ds(0, 16)], wg1.at[chip, core], w1_send.at[k], w1_recv.at[k], dp=peer(k))
+        return remote(wsend.at[pl.ds(0, 16)], wg1.at[chip, core], w1_send, w1_recv, dp=peer(k))
 
     def w2_copy(k):
-        return remote(wsend.at[pl.ds(16, 64)], wg2.at[chip, core], w2_send.at[k], w2_recv.at[k], dp=peer(k))
-
+        return remote(wsend.at[pl.ds(16, 64)], wg2.at[chip, core], w2_send, w2_recv, dp=peer(k))
+
+    w1_all = whole(wg1.at[pl.ds(1, CHIPS - 1), 0], w1_send, w1_recv)
+    w2_all = whole(wg2.at[pl.ds(1, CHIPS - 1), 0], w2_send, w2_recv)
+    b1_all = whole(rb1.at[pl.ds(1, CHIPS - 1)], b1_send, b1_recv)
+    b2_all = whole(rb2.at[pl.ds(1, CHIPS - 1)], b2_send, b2_recv)
+    c1_all = whole(rc1.at[pl.ds(1, SP - 1)], c1_send, c1_recv)
+    c2_all = whole(rc2.at[pl.ds(1, SP - 1)], c2_send, c2_recv)
     each(1, CHIPS, lambda k: w1_copy(k).start())
     v_start, v_wait, v_drain = halo(0, vh.at[0], vh.at[1], vh.at[2], vh.at[3])
     v_start()
@@ -192,7 +201,7 @@
 
     each(0, X, lambda k: frame_input(vol[0, :, k], s1.at[k + 1]))
 
-    each(1, CHIPS, lambda k: w1_copy(k).wait_recv())
+    w1_all.wait_recv()
     forward1 = remote(wg1.at[:, core], wg1.at[:, core], pair_send.at[0], pair_recv.at[0], dp=sibling)
     forward1.start()
     v_wait()
@@ -207,23 +216,21 @@
 
     even = lax.rem(lanes(C1), 2) == 0
 
-    def first_layer(h):
-        for k in range(2):
-            x = 2 * h + k
-            pre1[k] = dot(w1t[...], s1[pl.ds(x, 3)].reshape(27 * C0, Y * Z))
+    for x in range(X):
+        pre1[x] = dot(w1t[...], s1[x : x + 3].reshape(27 * C0, Y * Z))
+    for h in range(2):
         for y in range(Y // 2):
             total = jnp.zeros((C1, Z), F32)
             for k in range(2):
                 for j in range(2):
                     at = slice((2 * y + j) * Z, (2 * y + j + 1) * Z)
-                    t = pre1[k, :, at]
+                    t = pre1[2 * h + k, :, at]
                     sigma = jax.nn.sigmoid(t)
                     total = total + t * sigma
                     slope1[2 * h + k, :, at] = sigma * (1.0 + t * (1.0 - sigma)) * 0.125
             other = jnp.where(even, pltpu.roll(total, Z - 1, 1), pltpu.roll(total, 1, 1))
             pp[h, y] = (total + other) * 0.125
 
-    each(0, 2, first_layer)
     for h in range(2):
         for y in range(2):
             ps[h, y] = jnp.where(even, pp[h, 2 * y], pp[h, 2 * y + 1]).astype(BF16)
@@ -236,7 +243,7 @@
             return jnp.where(even, wide, pltpu.roll(wide, 1, 1))
         return jnp.where(even, pltpu.roll(wide, Z - 1, 1), wide)
 
-    each(1, CHIPS, lambda k: w2_copy(k).wait_recv())
+    w2_all.wait_recv()
     forward2 = remote(wg2.at[:, core], wg2.at[:, core], pair_send.at[1], pair_recv.at[1], dp=sibling)
     forward2.start()
     for h in range(2):
@@ -273,9 +280,9 @@
         sums.append(total)
 
     for k in range(2):
-        taps2[0:576] = dot(w2[1152 * k : 1152 * k + 576], d2[k])
+        edge2[k] = dot(w2[1152 * k : 1152 * k + 576], d2[k])
         for y in range(2):
-            a, b = (gather_taps(taps2, C1, Y // 2, 2 * y + j, 2) for j in range(2))
+            a, b = (gather_taps(edge2.at[k], C1, Y // 2, 2 * y + j, 2) for j in range(2))
             es[k, y] = jnp.where(even, a, b).astype(BF16)
     e_start, e_wait, e_drain = halo(2, es.at[0], es.at[1], eh.at[0], eh.at[1])
     e_start()
@@ -297,8 +304,6 @@
         high = total.astype(BF16)
         low = (total - high.astype(F32)).astype(BF16)
         pooled_out[y] = (dot_nt(squeeze, high) + dot_nt(squeeze, low)).astype(BF16)
-    store_pooled = pltpu.make_async_copy(pooled_out, pooled_to, out_sem.at[X])
-    store_pooled.start()
 
     pair2.wait_recv()
 
@@ -309,7 +314,7 @@
 
     def b2_copy(k):
         return remote(
-            pb2.at[lax.rem(chip + k, CHIPS)], rb2.at[k], b2_send.at[k], b2_recv.at[k], dp=peer(k)
+            pb2.at[lax.rem(chip + k, CHIPS)], rb2.at[k], b2_send, b2_recv, dp=peer(k)
         )
 
     each(1, CHIPS, lambda k: b2_copy(k).start())
@@ -327,10 +332,9 @@
                     at = slice((2 * y + j) * Z, (2 * y + j + 1) * Z)
                     d1[2 * x + k + 2, :, at] = (grad * slope1[2 * x + k, :, at]).astype(BF16)
 
-    def add_plane(k, acc):
-        return acc + dot_nt(s1[k], d1[pl.ds(k, 3)].reshape(3 * C1, Y * Z))
-
-    acc = lax.fori_loop(0, X + 2, add_plane, jnp.zeros((9 * C0, 3 * C1), F32))
+    acc = dot_nt(s1[0], d1[0:3].reshape(3 * C1, Y * Z))
+    for k in range(1, X + 2):
+        acc = acc + dot_nt(s1[k], d1[k : k + 3].reshape(3 * C1, Y * Z))
     for a in range(3):
         gs1[a * 288 : (a + 1) * 288, :] = acc[:, (2 - a) * C1 : (3 - a) * C1]
     for k in range(DP):
@@ -343,9 +347,9 @@
     pair1.start()
 
     for k in range(2):
-        taps1[...] = dot(w1[576 * k : 576 * k + 288], d1[2 + (X - 1) * k])
+        taps1[k] = dot(w1[576 * k : 576 * k + 288], d1[2 + (X - 1) * k])
         for y in range(Y):
-            fs[k, y] = gather_taps(taps1, C0, Y, y, 1).astype(BF16)
+            fs[k, y] = gather_taps(taps1.at[k], C0, Y, y, 1).astype(BF16)
     f_start, f_wait, f_drain = halo(3, fs.at[0], fs.at[1], fh.at[0], fh.at[1])
     f_start()
 
@@ -358,87 +362,76 @@
 
     def b1_copy(k):
         return remote(
-            pb1.at[lax.rem(chip + k, CHIPS)], rb1.at[k], b1_send.at[k], b1_recv.at[k], dp=peer(k)
+            pb1.at[lax.rem(chip + k, CHIPS)], rb1.at[k], b1_send, b1_recv, dp=peer(k)
         )
 
     each(1, CHIPS, lambda k: b1_copy(k).start())
 
     left1 = jnp.concatenate([w1[576:864], w1[288:576], w1[0:288]], axis=1)
 
-    def store_vgrad(x):
-        return pltpu.make_async_copy(vgrad_out.at[x], vgrad_to.at[0, :, x], out_sem.at[x])
-
     def volume_grad(x, extra=None):
-        taps1[...] = dot(left1, d1[pl.ds(x + 1, 3)].reshape(3 * C1, Y * Z))
+        taps1[x] = dot(left1, d1[x + 1 : x + 4].reshape(3 * C1, Y * Z))
         for y in range(Y):
-            piece = gather_taps(taps1, C0, Y, y, 1)
+            piece = gather_taps(taps1.at[x], C0, Y, y, 1)
             if extra is not None:
                 piece = piece + extra[y].astype(F32)
-            fst[pl.ds(y, C0, stride=Y), :] = piece
-        vgrad_out[x] = fst[...].reshape(C0, Y, Z).astype(BF16)
-        store_vgrad(x).start()
-
-    each(1, X - 1, volume_grad)
-    each(1, CHIPS, lambda k: b2_copy(k).wait_recv())
+            grow[x, pl.ds(y, C0, stride=Y), :] = piece
+        vgrad_out[x] = grow[x].reshape(C0, Y, Z).astype(BF16)
+
+    for x in range(1, X - 1):
+        volume_grad(x)
+    b2_all.wait_recv()
     sum2 = lax.fori_loop(1, CHIPS, lambda k, t: t + rb2[k].astype(F32), pb2[chip].astype(F32))
     sc2[...] = sum2.astype(BF16)
 
     def c2_copy(k):
-        return remote(sc2, rc2.at[k], c2_send.at[k], c2_recv.at[k], space=lax.rem(s + k, SP))
+        return remote(sc2, rc2.at[k], c2_send, c2_recv, space=lax.rem(s + k, SP))
 
     each(1, SP, lambda k: c2_copy(k).start())
     f_wait()
-    each(0, 2, lambda k: volume_grad((X - 1) * k, fh.at[k]))
-
-    each(1, CHIPS, lambda k: b1_copy(k).wait_recv())
+    for k in range(2):
+        volume_grad((X - 1) * k, fh.at[k])
+
+    b1_all.wait_recv()
     sum1 = lax.fori_loop(1, CHIPS, lambda k, t: t + rb1[k].astype(F32), pb1[chip].astype(F32))
     sc1[...] = sum1.astype(BF16)
 
     def c1_copy(k):
-        return remote(sc1, rc1.at[k], c1_send.at[k], c1_recv.at[k], space=lax.rem(s + k, SP))
+        return remote(sc1, rc1.at[k], c1_send, c1_recv, space=lax.rem(s + k, SP))
 
     each(1, SP, lambda k: c1_copy(k).start())
-    each(1, SP, lambda k: c2_copy(k).wait_recv())
+    c2_all.wait_recv()
     full2 = lax.fori_loop(1, SP, lambda k, t: t + rc2[k].astype(F32), sc2[...].astype(F32))
     gtwo_out[...] = full2[0:R2] * (0.5 * FACTOR_TWO)
-    store_gtwo = pltpu.make_async_copy(gtwo_out, gtwo_to, out_sem.at[X + 1])
-    store_gtwo.start()
 
     v_drain()
     p_drain()
     e_drain()
     f_drain()
-    each(1, CHIPS, lambda k: w1_copy(k).wait_send())
-    each(1, CHIPS, lambda k: w2_copy(k).wait_send())
-    each(1, CHIPS, lambda k: b2_copy(k).wait_send())
-    each(1, CHIPS, lambda k: b1_copy(k).wait_send())
+    w1_all.wait_send()
+    w2_all.wait_send()
+    b2_all.wait_send()
+    b1_all.wait_send()
     forward1.wait_send()
     forward2.wait_send()
     pair1.wait_send()
     pair2.wait_send()
-    each(1, SP, lambda k: c2_copy(k).wait_send())
-    each(1, SP, lambda k: c1_copy(k).wait_send())
-
-    each(1, SP, lambda k: c1_copy(k).wait_recv())
+    c2_all.wait_send()
+    c1_all.wait_send()
+
+    c1_all.wait_recv()
     full1 = lax.fori_loop(1, SP, lambda k, t: t + rc1[k].astype(F32), sc1[...].astype(F32))
     gone_out[0:16, :] = full1[:, 0:C1] * FACTOR_ONE
     gone_out[16:R1, :] = pltpu.roll(full1, 64, 1)[0 : R1 - 16, 0:C1] * FACTOR_ONE
-    store_gone = pltpu.make_async_copy(gone_out, gone_to, out_sem.at[X + 2])
-    store_gone.start()
-    each(0, X, lambda k: store_vgrad(k).wait())
-    store_pooled.wait()
-    store_gtwo.wait()
-    store_gone.wait()
-
-
-def hand_over(*refs):
-    sources, dests, held, sem = refs[0:4], refs[4:8], refs[8:12], refs[12]
-    loads = [pltpu.make_async_copy(sources[k], held[k], sem.at[0, k]) for k in range(4)]
-    stores = [pltpu.make_async_copy(held[k], dests[k], sem.at[1, k]) for k in range(4)]
-    for load in loads:
-        load.start()
-    for load, store in zip(loads, stores):
-        load.wait()
+
+
+def hand_over(pooled, vgrad, gone, gtwo, pooled_to, vgrad_to, gone_to, gtwo_to, sem):
+    stores = [pltpu.make_async_copy(vgrad.at[x], vgrad_to.at[0, :, x], sem.at[x]) for x in range(X)]
+    stores += [
+        pltpu.make_async_copy(src, dst, sem.at[X + k])
+        for k, (src, dst) in enumerate(((pooled, pooled_to), (gone, gone_to), (gtwo, gtwo_to)))
+    ]
+    for store in stores:
         store.start()
     for store in stores:
         store.wait()
@@ -454,16 +447,18 @@
         jax.ShapeDtypeStruct((R2, C2), F32),
     )
     dma = pltpu.SemaphoreType.DMA
+    vmem = pl.BlockSpec(memory_space=pltpu.VMEM)
     results = pl.pallas_call(
         kernel,
-        out_shape=shapes,
-        in_specs=[hbm] * 4,
-        out_specs=(hbm,) * 4,
-        scratch_shapes=[
+        out_shape=(
             pltpu.VMEM((2, 32, C2), BF16),
             pltpu.VMEM((X, C0, Y, Z), BF16),
             pltpu.VMEM((R1, C1), F32),
             pltpu.VMEM((R2, C2), F32),
+        ),
+        in_specs=[hbm] * 4,
+        out_specs=(vmem,) * 4,
+        scratch_shapes=[
             pltpu.VMEM((1, C0, X, Y, Z), BF16),
             pltpu.VMEM((R1, C1), BF16),
             pltpu.VMEM((R2, C2), BF16),
@@ -471,7 +466,7 @@
             pltpu.VMEM((4, C0, Y, Z), BF16),
             pltpu.VMEM((C0 * Y, Z), F32),
             pltpu.VMEM((X + 2, 9 * C0, Y * Z), BF16),
-            pltpu.VMEM((2, C1, Y * Z), F32),
+            pltpu.VMEM((X, C1, Y * Z), F32),
             pltpu.VMEM((X, C1, Y * Z), F32),
             pltpu.VMEM((2, Y // 2, C1, Z), F32),
             pltpu.VMEM((2, 2, C1, Z), BF16),
@@ -482,8 +477,10 @@
             pltpu.VMEM((2, 2, C1, Z), BF16),
             pltpu.VMEM((2, 2, C1, Z), BF16),
             pltpu.VMEM((X + 4, C1, Y * Z), BF16),
-            pltpu.VMEM((9 * C0, Y * Z), F32),
+            pltpu.VMEM((X, 9 * C0, Y * Z), F32),
+            pltpu.VMEM((X, C0 * Y, Z), F32),
             pltpu.VMEM((18 * C1, Y // 2 * Z), F32),
+            pltpu.VMEM((2, 9 * C1, Y // 2 * Z), F32),
             pltpu.VMEM((2, Y, C0, Z), BF16),
             pltpu.VMEM((2, Y, C0, Z), BF16),
             pltpu.VMEM((32, C1), F32),
@@ -510,26 +507,26 @@
             pltpu.VMEM((64, 128), BF16),
             pltpu.VMEM((SP, 16, 128), BF16),
             pltpu.VMEM((SP, 64, 128), BF16),
-            dma((4,)), dma((X + 3,)),
+            dma((4,)),
             dma((4, 2)), dma((4, 2)),
             dma((4,)), dma((4,)),
-            dma((CHIPS,)), dma((CHIPS,)),
-            dma((CHIPS,)), dma((CHIPS,)),
-            dma((CHIPS,)), dma((CHIPS,)),
-            dma((CHIPS,)), dma((CHIPS,)),
-            dma((SP,)), dma((SP,)),
-            dma((SP,)), dma((SP,)),
+            dma, dma,
+            dma, dma,
+            dma, dma,
+            dma, dma,
+            dma, dma,
+            dma, dma,
         ],
         compiler_params=pltpu.CompilerParams(
             collective_id=0, has_side_effects=True, vmem_limit_bytes=VMEM_BYTES
         ),
-    )(volumes, w_first, w_second, cot)
+    )(*(pltpu.with_memory_space_constraint(each, pltpu.HBM) for each in (volumes, w_first, w_second, cot)))
     pooled, vgrad, gone, gtwo = pl.pallas_call(
         hand_over,
         out_shape=shapes,
-        in_specs=[hbm] * 4,
+        in_specs=[vmem] * 4,
         out_specs=(hbm,) * 4,
-        scratch_shapes=[*(pltpu.VMEM(each.shape, each.dtype) for each in shapes), dma((2, 4))],
+        scratch_shapes=[dma((X + 3,))],
         compiler_params=pltpu.CompilerParams(vmem_limit_bytes=VMEM_BYTES),
     )(*results)
     return (pooled.transpose(2, 0, 1)[None, :, None], vgrad, gone, gtwo)

time: 49.8 us -> 46.4 us (0.932)
  Pallas kernels: 48.9 us -> 45.6 us
    pallas_call x2, Pallas kernels: 48.9 us -> 45.6 us  [the longest x1 44.8 us: local(): pl.pallas_call(kernel, out_shape=(pltpu.VMEM((2, 32, C2), BF16), pltpu.VM...]
where the time goes in v3:
time: 46.4 us; the launch traced here: 46.3 us
  Pallas kernels  45.6 us (98%)
  between operations  0.64 us (1%)
    pallas_call x1, Pallas kernels, local(): pl.pallas_call(kernel, out_shape=(pltpu.VMEM((2, 32, C2), BF16), pltpu.VM...  44.8 us

profile of v3, /device:TPU:1, one launch (start us, length us, event | category | flops | bytes accessed | tf_op | source)
XLA Modules:
  0.0 46.3 jit_solution(9019273403677266491)
XLA Ops:
  0.6 44.8 %shard_map.75 = (bf16[2,32,128]{2,1,0:T(8,128)(2,1)S(1)}, bf16[4,32,8,128]{3,2,1,0:T(8,128)(2,1)S(1)}, f32[27,64]{1,0:T(8,128)S(1)}, f32[54,128]{1,0:T(8,128)S(1)}) custom-call(bf16[1,32,4,8,128]{4,3,2,1,0:T(8,128)(2,1)} %vol_in.1, bf16[27,64]{1,0:T(8,128)(2,1)} %wone_in.1, bf16[54,128]{1,0:T(8,128)(2,1)} %wtwo_in.1, bf16[2,32,128]{2,1,0:T(8,128)(2,1)} %bitcast.6), custom_call_target="tpu_custom_call" | custom-call | tf_op jit(solution)/shard_map/pallas_call | solution.py:451
  45.5 0.8 %shard_map.76 = (bf16[2,32,128]{2,1,0:T(8,128)(2,1)}, bf16[1,32,4,8,128]{4,3,2,1,0:T(8,128)(2,1)}, f32[27,64]{1,0:T(8,128)}, f32[54,128]{1,0:T(8,128)}) custom-call(bf16[2,32,128]{2,1,0:T(8,128)(2,1)S(1)} %get-tuple-element.12.pooled, bf16[4,32,8,128]{3,2,1,0:T(8,128)(2,1)S(1)} %get-tuple-element.13.vgrad, f32[27,64]{1,0:T(8,128)S(1)} %get-tuple-element.14.gone, ...), custom_call_target="tpu_custom_call" | custom-call | tf_op jit(solution)/shard_map/pallas_call | solution.py:524

commit v4 on v3

--- a/solution.py
+++ b/solution.py
@@ -287,8 +287,9 @@
     e_start, e_wait, e_drain = halo(2, es.at[0], es.at[1], eh.at[0], eh.at[1])
     e_start()
 
+    parts = [dot_nt(s2[k], d2[...].reshape(2 * C2, Y // 2 * Z)) for k in range(4)]
     for a in range(3):
-        gs2[a * 576 : (a + 1) * 576, :] = dot_nt(s2[a], d2[0]) + dot_nt(s2[a + 1], d2[1])
+        gs2[a * 576 : (a + 1) * 576, :] = parts[a][:, 0:128] + parts[a + 1][:, 128:256]
     for k in range(DP):
         gp2[k // 2, k % 2, 0:R2, :] = gs2[R2 * k : R2 * k + R2, :].astype(BF16)
         gp2[k // 2, k % 2, R2:64, :] = jnp.zeros((64 - R2, C2), BF16)
@@ -321,8 +322,7 @@
 
     e_wait()
     for k in range(2):
-        d1[k] = jnp.zeros((C1, Y * Z), BF16)
-        d1[X + 2 + k] = jnp.zeros((C1, Y * Z), BF16)
+        d1[1 + (X + 1) * k] = jnp.zeros((C1, Y * Z), BF16)
     for x in range(2):
         for y in range(Y // 2):
             grad = gather_taps(taps2.at[x * 576 : (x + 1) * 576], C1, Y // 2, y, 2) + apart(eh[x], y)
@@ -332,11 +332,11 @@
                     at = slice((2 * y + j) * Z, (2 * y + j + 1) * Z)
                     d1[2 * x + k + 2, :, at] = (grad * slope1[2 * x + k, :, at]).astype(BF16)
 
-    acc = dot_nt(s1[0], d1[0:3].reshape(3 * C1, Y * Z))
-    for k in range(1, X + 2):
-        acc = acc + dot_nt(s1[k], d1[k : k + 3].reshape(3 * C1, Y * Z))
+    parts = [dot_nt(s1[k], d1[2 : X + 2].reshape(X * C1, Y * Z)) for k in range(X + 2)]
     for a in range(3):
-        gs1[a * 288 : (a + 1) * 288, :] = acc[:, (2 - a) * C1 : (3 - a) * C1]
+        low = parts[a][:, 0:128] + parts[a + 2][:, 128:256]
+        high = parts[a + 1][:, 0:128] + parts[a + 3][:, 128:256]
+        gs1[a * 288 : (a + 1) * 288, :] = (low + pltpu.roll(high, 64, 1))[:, 0:C1]
     for k in range(DP):
         head = gs1[R1 * k : R1 * k + 16, :].astype(BF16)
         tail = jnp.concatenate(

time: 46.4 us -> 45.5 us (0.981)
  Pallas kernels: 45.6 us -> 44.7 us
    pallas_call x1, Pallas kernels: 44.8 us -> 44 us  [local(): pl.pallas_call(kernel, out_shape=(pltpu.VMEM((2, 32, C2), BF16), pltpu.VM...]
where the time goes in v4:
time: 45.5 us; the launch traced here: 45.4 us
  Pallas kernels  44.7 us (98%)
  between operations  0.64 us (1%)
    pallas_call x1, Pallas kernels, local(): pl.pallas_call(kernel, out_shape=(pltpu.VMEM((2, 32, C2), BF16), pltpu.VM...  44 us

profile of v4, /device:TPU:1, one launch (start us, length us, event | category | flops | bytes accessed | tf_op | source)
XLA Modules:
  0.0 45.4 jit_solution(17865087909865440446)
XLA Ops:
  0.6 44.0 %shard_map.75 = (bf16[2,32,128]{2,1,0:T(8,128)(2,1)S(1)}, bf16[4,32,8,128]{3,2,1,0:T(8,128)(2,1)S(1)}, f32[27,64]{1,0:T(8,128)S(1)}, f32[54,128]{1,0:T(8,128)S(1)}) custom-call(bf16[1,32,4,8,128]{4,3,2,1,0:T(8,128)(2,1)} %vol_in.1, bf16[27,64]{1,0:T(8,128)(2,1)} %wone_in.1, bf16[54,128]{1,0:T(8,128)(2,1)} %wtwo_in.1, bf16[2,32,128]{2,1,0:T(8,128)(2,1)} %bitcast.6), custom_call_target="tpu_custom_call" | custom-call | tf_op jit(solution)/shard_map/pallas_call | solution.py:451
  44.6 0.8 %shard_map.76 = (bf16[2,32,128]{2,1,0:T(8,128)(2,1)}, bf16[1,32,4,8,128]{4,3,2,1,0:T(8,128)(2,1)}, f32[27,64]{1,0:T(8,128)}, f32[54,128]{1,0:T(8,128)}) custom-call(bf16[2,32,128]{2,1,0:T(8,128)(2,1)S(1)} %get-tuple-element.12.pooled, bf16[4,32,8,128]{3,2,1,0:T(8,128)(2,1)S(1)} %get-tuple-element.13.vgrad, f32[27,64]{1,0:T(8,128)S(1)} %get-tuple-element.14.gone, ...), custom_call_target="tpu_custom_call" | custom-call | tf_op jit(solution)/shard_map/pallas_call | solution.py:524

commit v5 on v4

--- a/solution.py
+++ b/solution.py
@@ -18,6 +18,7 @@
 X, Y, Z = 4, 8, 128
 R1, R2 = 27, 54
 VMEM_BYTES = 48 * 1024 * 1024
+FAR_CHIPS = (12, 11, 13, 4, 10, 14, 3, 5, 9, 15, 2, 6, 8, 1, 7)
 FACTOR_ONE = float(1048576) ** (-0.5)
 FACTOR_TWO = float(131072) ** (-0.5)
 
@@ -190,10 +191,12 @@
     b2_all = whole(rb2.at[pl.ds(1, CHIPS - 1)], b2_send, b2_recv)
     c1_all = whole(rc1.at[pl.ds(1, SP - 1)], c1_send, c1_recv)
     c2_all = whole(rc2.at[pl.ds(1, SP - 1)], c2_send, c2_recv)
-    each(1, CHIPS, lambda k: w1_copy(k).start())
+    for k in FAR_CHIPS:
+        w1_copy(k).start()
     v_start, v_wait, v_drain = halo(0, vh.at[0], vh.at[1], vh.at[2], vh.at[3])
     v_start()
-    each(1, CHIPS, lambda k: w2_copy(k).start())
+    for k in FAR_CHIPS:
+        w2_copy(k).start()
 
     def frame_input(plane, dest):
         fst[...] = plane.astype(F32).reshape(C0 * Y, Z)

time: 45.5 us -> 43.8 us (0.963)
  Pallas kernels: 44.7 us -> 43.1 us
    pallas_call x1, Pallas kernels: 44 us -> 42.3 us  [local(): pl.pallas_call(kernel, out_shape=(pltpu.VMEM((2, 32, C2), BF16), pltpu.VM...]
where the time goes in v5:
time: 43.8 us; the launch traced here: 43.7 us
  Pallas kernels  43.1 us (98%)
  between operations  0.64 us (1%)
    pallas_call x1, Pallas kernels, local(): pl.pallas_call(kernel, out_shape=(pltpu.VMEM((2, 32, C2), BF16), pltpu.VM...  42.3 us

profile of v5, /device:TPU:1, one launch (start us, length us, event | category | flops | bytes accessed | tf_op | source)
XLA Modules:
  0.0 43.7 jit_solution(14036602723609966596)
XLA Ops:
  0.6 42.3 %shard_map.75 = (bf16[2,32,128]{2,1,0:T(8,128)(2,1)S(1)}, bf16[4,32,8,128]{3,2,1,0:T(8,128)(2,1)S(1)}, f32[27,64]{1,0:T(8,128)S(1)}, f32[54,128]{1,0:T(8,128)S(1)}) custom-call(bf16[1,32,4,8,128]{4,3,2,1,0:T(8,128)(2,1)} %vol_in.1, bf16[27,64]{1,0:T(8,128)(2,1)} %wone_in.1, bf16[54,128]{1,0:T(8,128)(2,1)} %wtwo_in.1, bf16[2,32,128]{2,1,0:T(8,128)(2,1)} %bitcast.6), custom_call_target="tpu_custom_call" | custom-call | tf_op jit(solution)/shard_map/pallas_call | solution.py:454
  42.9 0.8 %shard_map.76 = (bf16[2,32,128]{2,1,0:T(8,128)(2,1)}, bf16[1,32,4,8,128]{4,3,2,1,0:T(8,128)(2,1)}, f32[27,64]{1,0:T(8,128)}, f32[54,128]{1,0:T(8,128)}) custom-call(bf16[2,32,128]{2,1,0:T(8,128)(2,1)S(1)} %get-tuple-element.12.pooled, bf16[4,32,8,128]{3,2,1,0:T(8,128)(2,1)S(1)} %get-tuple-element.13.vgrad, f32[27,64]{1,0:T(8,128)S(1)} %get-tuple-element.14.gone, ...), custom_call_target="tpu_custom_call" | custom-call | tf_op jit(solution)/shard_map/pallas_call | solution.py:527

commit v6 on v5

--- a/solution.py
+++ b/solution.py
@@ -321,7 +321,8 @@
             pb2.at[lax.rem(chip + k, CHIPS)], rb2.at[k], b2_send, b2_recv, dp=peer(k)
         )
 
-    each(1, CHIPS, lambda k: b2_copy(k).start())
+    for k in FAR_CHIPS:
+        b2_copy(k).start()
 
     e_wait()
     for k in range(2):
@@ -368,7 +369,8 @@
             pb1.at[lax.rem(chip + k, CHIPS)], rb1.at[k], b1_send, b1_recv, dp=peer(k)
         )
 
-    each(1, CHIPS, lambda k: b1_copy(k).start())
+    for k in FAR_CHIPS:
+        b1_copy(k).start()
 
     left1 = jnp.concatenate([w1[576:864], w1[288:576], w1[0:288]], axis=1)
 

time: 43.8 us -> 44.1 us (level)
  no operation moved by 1% of the time
where the time goes in v6:
time: 44.1 us; the launch traced here: 43.9 us
  Pallas kernels  43.2 us (98%)
  between operations  0.64 us (1%)
    pallas_call x1, Pallas kernels, local(): pl.pallas_call(kernel, out_shape=(pltpu.VMEM((2, 32, C2), BF16), pltpu.VM...  42.5 us

profile of v6, /device:TPU:1, one launch (start us, length us, event | category | flops | bytes accessed | tf_op | source)
XLA Modules:
  0.0 43.9 jit_solution(5102586700718198588)
XLA Ops:
  0.6 42.5 %shard_map.75 = (bf16[2,32,128]{2,1,0:T(8,128)(2,1)S(1)}, bf16[4,32,8,128]{3,2,1,0:T(8,128)(2,1)S(1)}, f32[27,64]{1,0:T(8,128)S(1)}, f32[54,128]{1,0:T(8,128)S(1)}) custom-call(bf16[1,32,4,8,128]{4,3,2,1,0:T(8,128)(2,1)} %vol_in.1, bf16[27,64]{1,0:T(8,128)(2,1)} %wone_in.1, bf16[54,128]{1,0:T(8,128)(2,1)} %wtwo_in.1, bf16[2,32,128]{2,1,0:T(8,128)(2,1)} %bitcast.6), custom_call_target="tpu_custom_call" | custom-call | tf_op jit(solution)/shard_map/pallas_call | solution.py:456
  43.1 0.8 %shard_map.76 = (bf16[2,32,128]{2,1,0:T(8,128)(2,1)}, bf16[1,32,4,8,128]{4,3,2,1,0:T(8,128)(2,1)}, f32[27,64]{1,0:T(8,128)}, f32[54,128]{1,0:T(8,128)}) custom-call(bf16[2,32,128]{2,1,0:T(8,128)(2,1)S(1)} %get-tuple-element.12.pooled, bf16[4,32,8,128]{3,2,1,0:T(8,128)(2,1)S(1)} %get-tuple-element.13.vgrad, f32[27,64]{1,0:T(8,128)S(1)} %get-tuple-element.14.gone, ...), custom_call_target="tpu_custom_call" | custom-call | tf_op jit(solution)/shard_map/pallas_call | solution.py:529
